TPU v7x, 32 devices: a whole 2x2x4 slice. The times are simulated.
32 devices in a mesh: ra: 8 (over z, x), dec: 4 (over y, core).
Axes of the slice: x: 2, y: 2, z: 4, core: 2. Of those that a mesh axis runs over, the one named last changes fastest.
Arguments:
- lens_block: bfloat16 [8, 4, 130, 512], P('ra', 'dec'), may hold values from 0 to 255, as said below
- lens_count: int32 [8, 4], P('ra', 'dec'), may hold values from 64 to 512, as said below
- lens_region: int32 [8, 4, 512], P('ra', 'dec'), may hold values from 0 to 255, as said below
- lens_sample: int32 [8, 4, 512], P('ra', 'dec'), may hold values from 0 to 7
- source_block: bfloat16 [8, 4, 133, 1024], P('ra', 'dec'), may hold values from -1 to 255, as said below
Outputs:
- jk_signal: float32 [256, 8, 20], P(('ra', 'dec'))
- jk_weight: float32 [256, 8, 20], P(('ra', 'dec'))
Inputs may be any that keep to these rules, and one draw needn't show every extreme that they name: The live lenses of patch (i, j) fill its first lens_count[i, j] slots; each count is 512, 256, 128 or 64, and at least one patch is full. `lens_block`: the first 128 rows are zero or positive, and zero below the lens's own redshift bin; the last two rows are whole numbers from 0 to 255. `source_block`: the first 128 rows are zero or positive; positions are whole numbers from 0 to 255; weights are positive. `lens_region`: each id labels a compact area of the sky.
All inputs are finite; a program needn't handle non-finite values.
Results may differ from a plain program's by a relative error of at most 0.0003.
Values may be sent and summed in bfloat16 or wider, within the bound.
A program may use at most 64 MiB of HBM per device.

v0:
```python
import math

import jax
import jax.numpy as jnp
from jax import lax
from jax.sharding import PartitionSpec as P

NBIN = 20
SAMPLES = 8
PATCH = 256
R_IN = 12
L_PATCH = 512
S_PATCH = 1024
REG_DEV = 8


growth_top = 23
growth_bottom = 20


def extended(block, sides, width, periodic):
    for axis, dim in sides:
        count = lax.axis_size(axis)
        forward = [(i, i + 1) for i in range(count - 1)]
        if periodic:
            forward.append((count - 1, 0))
        backward = [(target, source) for source, target in forward]
        low = lax.ppermute(
            lax.slice_in_dim(block, block.shape[dim] - width, None, axis=dim), axis, forward
        )
        high = lax.ppermute(lax.slice_in_dim(block, 0, width, axis=dim), axis, backward)
        block = jnp.concatenate([low, block, high], axis=dim)
    return block


def edge_squares():
    return [
        float((R_IN * growth_top**edge_level // growth_bottom**edge_level) ** 2)
        for edge_level in range(NBIN + 1)
    ]


def bin_scales():
    edge_sq = edge_squares()
    lens_per_cell = L_PATCH / (SAMPLES * REG_DEV)
    density = S_PATCH / (PATCH * PATCH)
    expected = [
        math.pi * (edge_sq[edge_level + 1] - edge_sq[edge_level]) * density * lens_per_cell
        for edge_level in range(NBIN)
    ]
    return jnp.array(expected, jnp.float32)


def pair_sums(kernel_tile, lens_x, lens_y, source_rows, edge_sq):
    pdf_bins = kernel_tile.shape[0]
    inverse_crit = lax.dot_general(
        kernel_tile,
        source_rows[:pdf_bins],
        (((0,), (0,)), ((), ())),
        preferred_element_type=jnp.float32,
    )
    catalog = source_rows[pdf_bins:].astype(jnp.float32)
    delta_x = catalog[0][None, :] - lens_x[:, None]
    delta_y = catalog[1][None, :] - lens_y[:, None]
    radius_sq = delta_x * delta_x + delta_y * delta_y
    safe_sq = jnp.maximum(radius_sq, edge_sq[0])
    cos_two = (delta_x * delta_x - delta_y * delta_y) / safe_sq
    sin_two = 2.0 * delta_x * delta_y / safe_sq
    tangent = -(catalog[2][None, :] * cos_two + catalog[3][None, :] * sin_two)
    weighted = catalog[4][None, :] * inverse_crit
    signal = weighted * tangent
    weight = weighted * inverse_crit
    lower_sq = jnp.array(edge_sq[:-1], jnp.float32)[:, None, None]
    upper_sq = jnp.array(edge_sq[1:], jnp.float32)[:, None, None]
    inside = (radius_sq[None] >= lower_sq) & (radius_sq[None] < upper_sq)
    signal_bins = jnp.sum(jnp.where(inside, signal[None], 0.0), axis=2)
    weight_bins = jnp.sum(jnp.where(inside, weight[None], 0.0), axis=2)
    return jnp.stack([signal_bins, weight_bins], axis=0)


def local_terms(lens_tile, neighbours, edge_sq):
    pdf_bins = lens_tile.shape[0] - 2
    kernel_tile = lens_tile[:pdf_bins]
    lens_x = lens_tile[pdf_bins].astype(jnp.float32)
    lens_y = lens_tile[pdf_bins + 1].astype(jnp.float32)
    totals = jnp.zeros((2, len(edge_sq) - 1, lens_tile.shape[1]), jnp.float32)
    for shift_x in (-1, 0, 1):
        for shift_y in (-1, 0, 1):
            source_rows = neighbours[3 * (shift_x + 1) + shift_y + 1]
            totals = totals + pair_sums(
                kernel_tile,
                lens_x - shift_x * PATCH,
                lens_y - shift_y * PATCH,
                source_rows,
                edge_sq,
            )
    return totals


def source_plan(lenses, beside_all, edge_sq, tile_rows):
    lens_total = lenses.shape[1]
    neighbours = [beside_all[shift_x, shift_y] for shift_x in range(3) for shift_y in range(3)]

    def tile_step(tile_index, totals):
        first_lens = tile_index * tile_rows
        lens_tile = lax.dynamic_slice_in_dim(lenses, first_lens, tile_rows, 1)
        tile_terms = local_terms(lens_tile, neighbours, edge_sq)
        return lax.dynamic_update_slice_in_dim(totals, tile_terms, first_lens, 2)

    empty_sums = jnp.zeros((2, NBIN, lens_total), jnp.float32)
    return lax.fori_loop(0, lens_total // tile_rows, tile_step, empty_sums)


def on_device(lens_block, lens_count, lens_region, lens_sample, source_block):
    edge_sq = edge_squares()
    lenses = lens_block[0, 0]
    lens_total = lenses.shape[1]
    tile_rows = math.gcd(lens_total, 128)
    live_count = lens_count[0, 0]
    partial_rows = extended(source_block, (("ra", 0),), 1, True)
    beside_all = extended(partial_rows, (("dec", 1),), 1, False)
    totals = source_plan(lenses, beside_all, edge_sq, tile_rows)
    live_lens = jnp.arange(lens_total, dtype=jnp.int32) < live_count
    totals = jnp.where(live_lens[None, None, :], totals, 0.0)
    per_lens = jnp.transpose(totals.reshape(2 * NBIN, lens_total))
    segment = lens_region[0, 0] * SAMPLES + lens_sample[0, 0]
    regions_total = REG_DEV * lax.axis_size("ra") * lax.axis_size("dec")
    region_table = jax.ops.segment_sum(per_lens, segment, num_segments=regions_total * SAMPLES)
    region_table = region_table.reshape(regions_total, SAMPLES * 2 * NBIN)
    owned_rows = lax.psum_scatter(region_table, ("ra", "dec"), scatter_dimension=0, tiled=True)
    owned_rows = owned_rows.reshape(-1, SAMPLES, 2, NBIN)
    scales = bin_scales()
    return (owned_rows[:, :, 0, :] / jnp.sqrt(scales), owned_rows[:, :, 1, :] / scales)


def solution(mesh):
    placed = (
        P("ra", "dec", None, None),
        P("ra", "dec"),
        P("ra", "dec", None),
        P("ra", "dec", None),
        P("ra", "dec", None, None),
    )
    return jax.shard_map(
        on_device,
        mesh=mesh,
        in_specs=placed,
        out_specs=(P(("ra", "dec"), None, None), P(("ra", "dec"), None, None)),
        check_vma=False,
    )
```

profile of v0, /device:TPU:0, one launch (start us, length us, event | category | flops | bytes accessed | tf_op | source)
XLA Modules:
  0.0 368.4 jit_solution(10899867084985026511)
XLA Ops:
  7.2 3.0 collective-permute-start
  10.2 3.1 collective-permute-start.1
  13.3 9.1 %collective-permute-done = bf16[1,1,133,1024]{3,2,1,0:T(8,128)(2,1)S(1)} collective-permute-done((bf16[1,1,133,1024]{3,2,1,0:T(8,128)(2,1)}, bf16[1,1,133,1024]{3,2,1,0:T(8,128)(2,1)S(1)}, u32[]{:S(2)}, u32[]{:S(2)}) %collective-permute-start) | collective-permute-done | bytes 272416 | tf_op jit(solution)/shard_map/ppermute | solution.py:28
  23.1 1.7 constant_dynamic-update-slice_fusion.1
  24.8 0.8 constant_dynamic-update-slice_fusion
  25.6 1.3 collective-permute-start.2
  27.0 1.3 collective-permute-start.3
  29.2 3.9 %collective-permute-done.3 = bf16[3,1,133,1024]{3,2,1,0:T(8,128)(2,1)S(1)} collective-permute-done((bf16[3,1,133,1024]{3,2,1,0:T(8,128)(2,1)}, bf16[3,1,133,1024]{3,2,1,0:T(8,128)(2,1)S(1)}, u32[]{:S(2)}, u32[]{:S(2)}) %collective-permute-start.3) | collective-permute-done | bytes 817184 | tf_op jit(solution)/shard_map/ppermute | solution.py:31
  33.2 184.3 %while.18 = (s32[]{:T(128)}, f32[2,20,512]{2,1,0:T(8,128)S(1)}, bf16[133,1024]{1,0:T(8,128)(2,1)S(1)}, bf16[130,512]{1,0:T(8,128)(2,1)S(1)}, bf16[133,1024]{1,0:...) while((s32[]{:T(128)}, f32[2,20,512]{2,1,0:T(8,128)S(1)}, ...), condition=%wide.region_19.20_spmd.clone.clone, body=%wide.region_0.19_spmd.sunk.clone.clone.sunk | while | flops 488462080 | bytes 35383924 | solution.py:111
  33.7 0.8 multiply_multiply_fusion.24
  35.8 0.8 multiply_multiply_fusion.27
  36.6 18.2 %select_reduce_fusion.20 = (f32[20,128]{1,0:T(8,128)S(1)}, f32[20,128]{1,0:T(8,128)S(1)}, f32[20,128]{1,0:T(8,128)S(1)}, f32[20,128]{1,0:T(8,128)S(1)}, f32[20,1...) fusion(f32[128,1024]{1,0:T(8,128)S(1)} %get-tuple-element.1218, ...), kind=kLoop, calls=%fused_computation.4.clone.1 | loop fusion | flops 73379840 | bytes 6373536 | tf_op jit(solution)/shard_map/while/body/eval_jaxpr/reduce_sum | solution.py:76
  55.2 0.8 multiply_multiply_fusion.28
  56.5 22.7 %select_reduce_fusion.21 = (f32[20,128]{1,0:T(8,128)S(1)}, f32[20,128]{1,0:T(8,128)S(1)}, f32[20,128]{1,0:T(8,128)S(1)}, f32[20,128]{1,0:T(8,128)S(1)}, f32[20,1...) fusion(f32[128,1024]{1,0:T(8,128)S(1)} %get-tuple-element.1270,, ...), kind=kLoop, calls=%fused_computation.2.clone.1 | loop fusion | flops 91724800 | bytes 7966880 | tf_op jit(solution)/shard_map/while/body/eval_jaxpr/reduce_sum | solution.py:76
  79.7 0.8 multiply_multiply_fusion.24
  81.8 0.8 multiply_multiply_fusion.27
  82.6 18.2 %select_reduce_fusion.20 = (f32[20,128]{1,0:T(8,128)S(1)}, f32[20,128]{1,0:T(8,128)S(1)}, f32[20,128]{1,0:T(8,128)S(1)}, f32[20,128]{1,0:T(8,128)S(1)}, f32[20,1...) fusion(f32[128,1024]{1,0:T(8,128)S(1)} %get-tuple-element.1218, ...), kind=kLoop, calls=%fused_computation.4.clone.1 | loop fusion | flops 73379840 | bytes 6373536 | tf_op jit(solution)/shard_map/while/body/eval_jaxpr/reduce_sum | solution.py:76
  101.2 0.8 multiply_multiply_fusion.28
  102.5 22.7 %select_reduce_fusion.21 = (f32[20,128]{1,0:T(8,128)S(1)}, f32[20,128]{1,0:T(8,128)S(1)}, f32[20,128]{1,0:T(8,128)S(1)}, f32[20,128]{1,0:T(8,128)S(1)}, f32[20,1...) fusion(f32[128,1024]{1,0:T(8,128)S(1)} %get-tuple-element.1270,, ...), kind=kLoop, calls=%fused_computation.2.clone.1 | loop fusion | flops 91724800 | bytes 7966880 | tf_op jit(solution)/shard_map/while/body/eval_jaxpr/reduce_sum | solution.py:76
  125.7 0.8 multiply_multiply_fusion.24
  127.9 0.8 multiply_multiply_fusion.27
  128.7 18.2 %select_reduce_fusion.20 = (f32[20,128]{1,0:T(8,128)S(1)}, f32[20,128]{1,0:T(8,128)S(1)}, f32[20,128]{1,0:T(8,128)S(1)}, f32[20,128]{1,0:T(8,128)S(1)}, f32[20,1...) fusion(f32[128,1024]{1,0:T(8,128)S(1)} %get-tuple-element.1218, ...), kind=kLoop, calls=%fused_computation.4.clone.1 | loop fusion | flops 73379840 | bytes 6373536 | tf_op jit(solution)/shard_map/while/body/eval_jaxpr/reduce_sum | solution.py:76
  147.2 0.8 multiply_multiply_fusion.28
  148.6 22.7 %select_reduce_fusion.21 = (f32[20,128]{1,0:T(8,128)S(1)}, f32[20,128]{1,0:T(8,128)S(1)}, f32[20,128]{1,0:T(8,128)S(1)}, f32[20,128]{1,0:T(8,128)S(1)}, f32[20,1...) fusion(f32[128,1024]{1,0:T(8,128)S(1)} %get-tuple-element.1270,, ...), kind=kLoop, calls=%fused_computation.2.clone.1 | loop fusion | flops 91724800 | bytes 7966880 | tf_op jit(solution)/shard_map/while/body/eval_jaxpr/reduce_sum | solution.py:76
  171.8 0.8 multiply_multiply_fusion.24
  173.9 0.8 multiply_multiply_fusion.27
  174.7 18.2 %select_reduce_fusion.20 = (f32[20,128]{1,0:T(8,128)S(1)}, f32[20,128]{1,0:T(8,128)S(1)}, f32[20,128]{1,0:T(8,128)S(1)}, f32[20,128]{1,0:T(8,128)S(1)}, f32[20,1...) fusion(f32[128,1024]{1,0:T(8,128)S(1)} %get-tuple-element.1218, ...), kind=kLoop, calls=%fused_computation.4.clone.1 | loop fusion | flops 73379840 | bytes 6373536 | tf_op jit(solution)/shard_map/while/body/eval_jaxpr/reduce_sum | solution.py:76
  193.3 0.8 multiply_multiply_fusion.28
  194.6 22.7 %select_reduce_fusion.21 = (f32[20,128]{1,0:T(8,128)S(1)}, f32[20,128]{1,0:T(8,128)S(1)}, f32[20,128]{1,0:T(8,128)S(1)}, f32[20,128]{1,0:T(8,128)S(1)}, f32[20,1...) fusion(f32[128,1024]{1,0:T(8,128)S(1)} %get-tuple-element.1270,, ...), kind=kLoop, calls=%fused_computation.2.clone.1 | loop fusion | flops 91724800 | bytes 7966880 | tf_op jit(solution)/shard_map/while/body/eval_jaxpr/reduce_sum | solution.py:76
  217.7 2.5 scatter_custom_fusion
  220.2 1.1 reshape.888
  221.3 138.6 %all-reduce.3.cloned.1.call-done = f32[256,320]{1,0:T(8,128)} async-done(((f32[256,320]{1,0:T(8,128)}), f32[256,320]{1,0:T(8,128)}) %all-reduce.3.cloned.1.call-update) | async-done | bytes 327696
  (129 shorter events, 12.6 us)
Async XLA Ops:
  7.2 21.8 %copy-start.6 = (s32[1,1,512]{2,1,0:T(1,128)S(1)}, s32[1,1,512]{2,1,0:T(1,128)}, u32[]{:S(2)}) copy-start(s32[1,1,512]{2,1,0:T(1,128)} %param.29) | copy-start | bytes 6148
  7.2 21.8 %copy-start.7 = (s32[1,1,512]{2,1,0:T(1,128)S(1)}, s32[1,1,512]{2,1,0:T(1,128)}, u32[]{:S(2)}) copy-start(s32[1,1,512]{2,1,0:T(1,128)} %param.28) | copy-start | bytes 6148
  7.2 352.8 %all-reduce.3.cloned.1.call-start = ((), (), s32[]{:S(2)}) async-start(), calls=%async_computation | async-start | bytes 786432
  7.2 15.2 %collective-permute-start = (bf16[1,1,133,1024]{3,2,1,0:T(8,128)(2,1)}, bf16[1,1,133,1024]{3,2,1,0:T(8,128)(2,1)S(1)}, u32[]{:S(2)}, u32[]{:S(2)}) collective-permute-start(bf16[1,1,133,1024]{3,2,1,0:T(8,128)(2,1)} %param.30), channel_id=1, source_target_pairs={{0,4},{4,8},{8,12},{12,16},{16,20},{20,24},{24,28},{28,0},{1,5},{5... | collective-permute-start | bytes 817160 | tf_op jit(solution)/shard_map/ppermute | solution.py:28
  10.2 14.6 %collective-permute-start.1 = (bf16[1,1,133,1024]{3,2,1,0:T(8,128)(2,1)}, bf16[1,1,133,1024]{3,2,1,0:T(8,128)(2,1)S(1)}, u32[]{:S(2)}, u32[]{:S(2)}) collective-permute-start(bf16[1,1,133,1024]{3,2,1,0:T(8,128)(2,1)} %param.30), channel_id=1, source_target_pairs={{4,0},{8,4},{12,8},{16,12},{20,16},{24,20},{28,24},{0,28},{5,1},{9... | collective-permute-start | bytes 817160 | tf_op jit(solution)/shard_map/ppermute | solution.py:31
  24.8 0.8 copy-start.2
  25.6 3.5 collective-permute-start.2
  27.0 6.2 %collective-permute-start.3 = (bf16[3,1,133,1024]{3,2,1,0:T(8,128)(2,1)}, bf16[3,1,133,1024]{3,2,1,0:T(8,128)(2,1)S(1)}, u32[]{:S(2)}, u32[]{:S(2)}) collective-permute-start(bf16[3,1,133,1024]{3,2,1,0:T(8,128)(2,1)} %constant_dynamic-update-slice_fusion), channel_id=1, source_target_pairs={{1,0},{2,1},{3,2},{5,4},{6,5},{7,6},{9,8},{10,9},{11,10},{13,12},{... | collective-permute-start | bytes 2451464 | tf_op jit(solution)/shard_map/ppermute | solution.py:31
  29.1 4.1 %copy-start = (bf16[1,1,133,1024]{3,2,1,0:T(8,128)(2,1)S(1)}, bf16[1,1,133,1024]{3,2,1,0:T(8,128)(2,1)}, u32[]{:S(2)}) copy-start(bf16[1,1,133,1024]{3,2,1,0:T(8,128)(2,1)} %param.30) | copy-start | bytes 817156
  29.2 4.1 %copy-start.1 = (bf16[1,1,130,512]{3,2,1,0:T(8,128)(2,1)S(1)}, bf16[1,1,130,512]{3,2,1,0:T(8,128)(2,1)}, u32[]{:S(2)}) copy-start(bf16[1,1,130,512]{3,2,1,0:T(8,128)(2,1)} %param.26) | copy-start | bytes 399364
  29.2 4.1 %copy-start.3 = (bf16[1,1,133,1024]{3,2,1,0:T(8,128)(2,1)S(1)}, bf16[1,1,133,1024]{3,2,1,0:T(8,128)(2,1)}, u32[]{:S(2)}) copy-start(bf16[1,1,133,1024]{3,2,1,0:T(8,128)(2,1)} %copy-done.2) | copy-start | bytes 817156
  29.2 4.1 %copy-start.4 = (f32[20]{0:T(128)S(1)}, f32[20]{0:T(128)}, u32[]{:S(2)}) copy-start(f32[20]{0:T(128)} %constant.113.clone..sunk.19) | copy-start | bytes 244
  29.2 4.1 %copy-start.5 = (f32[20]{0:T(128)S(1)}, f32[20]{0:T(128)}, u32[]{:S(2)}) copy-start(f32[20]{0:T(128)} %constant.112.clone..sunk.19) | copy-start | bytes 244
  220.2 140.7 %copy-start.8 = (f32[20]{0:T(128)S(1)}, f32[20]{0:T(128)}, u32[]{:S(2)}) copy-start(f32[20]{0:T(128)} %constant.122) | copy-start | bytes 244
  220.2 140.7 %copy-start.9 = (f32[20]{0:T(128)S(1)}, f32[20]{0:T(128)}, u32[]{:S(2)}) copy-start(f32[20]{0:T(128)} %constant.120) | copy-start | bytes 244
Sparse Core Ops, SparseCore 0:
  221.5 138.4 all-reduce.2
where the time goes:
time: 369 us; the launch traced here: 368 us
  other arithmetic  168 us (46%)
  waiting for transfers between devices  152 us (41%)
  matrix products  18.2 us (5%)
  between operations  14.9 us (4%)
  starting transfers between devices  8.76 us (2%)
  local copies, waits for them, and re-layouts  6.09 us (2%)
    reduce_sum x8, other arithmetic, pair_sums(): signal_bins = jnp.sum(jnp.where(inside, signal[None], 0.0), axis=2)  164 us
    unnamed x2, waiting for transfers between devices  139 us
    dot_general x36, matrix products, pair_sums(): lax.dot_general(kernel_tile, source_rows[:pdf_bins], (((0,), (0,)), ((),...  18.2 us
    ppermute x2, waiting for transfers between devices, extended(): lax.ppermute(lax.slice_in_dim(block, block.shape[dim] - width, None, axis...  9.22 us
  transfers between devices with their start and end apart: 5, of which 4 were waited for; matrix products, arithmetic and copies ran while one was open for 1% of the time, Pallas kernels for 0%

commit v1 on v0

v1 whole, which is shorter than its diff:
```python
import functools
import math

import jax
import jax.numpy as jnp
from jax import lax
from jax.experimental import pallas as pl
from jax.experimental.pallas import tpu as pltpu
from jax.sharding import PartitionSpec as P

NBIN = 20
SAMPLES = 8
PATCH = 256
R_IN = 12
L_PATCH = 512
S_PATCH = 1024
REG_DEV = 8


growth_top = 23
growth_bottom = 20


def extended(block, sides, width, periodic):
    for axis, dim in sides:
        count = lax.axis_size(axis)
        forward = [(i, i + 1) for i in range(count - 1)]
        if periodic:
            forward.append((count - 1, 0))
        backward = [(target, source) for source, target in forward]
        low = lax.ppermute(
            lax.slice_in_dim(block, block.shape[dim] - width, None, axis=dim), axis, forward
        )
        high = lax.ppermute(lax.slice_in_dim(block, 0, width, axis=dim), axis, backward)
        block = jnp.concatenate([low, block, high], axis=dim)
    return block


def edge_squares():
    return [
        float((R_IN * growth_top**edge_level // growth_bottom**edge_level) ** 2)
        for edge_level in range(NBIN + 1)
    ]


def bin_scales():
    edge_sq = edge_squares()
    lens_per_cell = L_PATCH / (SAMPLES * REG_DEV)
    density = S_PATCH / (PATCH * PATCH)
    expected = [
        math.pi * (edge_sq[edge_level + 1] - edge_sq[edge_level]) * density * lens_per_cell
        for edge_level in range(NBIN)
    ]
    return jnp.array(expected, jnp.float32)


def ranks(keys):
    total = keys.shape[0]
    unique = keys * total + jnp.arange(total, dtype=jnp.int32)
    return jnp.sum((unique[None, :] < unique[:, None]).astype(jnp.int32), axis=1)


def compact_order(position_x, position_y, dead, strip_size):
    strip = ranks(position_x + 2 * PATCH * dead) // strip_size
    return ranks(strip * (4 * PATCH) + position_y + 2 * PATCH * dead)


def pair_kernel(edge_sq, groups, chunk, class_ref, lens_ref, x_ref, y_ref, source_ref, catalog_ref, out_ref, crit, sums):
    patches, _, width = source_ref.shape
    tile = out_ref.shape[2]
    tiles = out_ref.shape[0]
    pieces = width // chunk

    def crit_step(patch, carry):
        crit[patch] = jnp.dot(lens_ref[...], source_ref[patch], preferred_element_type=jnp.float32)
        return carry

    lax.fori_loop(0, patches, crit_step, 0)

    def visit(first_edge, tile_index, patch, piece):
        rows = pl.ds(pl.multiple_of(tile_index * tile, tile), tile)
        lens_x = x_ref[rows, :]
        lens_y = y_ref[rows, :]
        parts = []
        for part in range(chunk // 128):
            columns = pl.ds(pl.multiple_of(piece * chunk + part * 128, 128), 128)
            inverse_crit = crit[patch, rows, columns]
            catalog = catalog_ref[patch, :, columns]
            delta_x = catalog[0:1] - lens_x
            delta_y = catalog[1:2] - lens_y
            square_x = delta_x * delta_x
            square_y = delta_y * delta_y
            radius_sq = square_x + square_y
            inverse = 1.0 / jnp.maximum(radius_sq, edge_sq[0])
            turned = catalog[2:3] * (square_x - square_y) + catalog[3:4] * (delta_x * delta_y)
            signal = inverse_crit * (turned * inverse)
            weight = catalog[4:5] * inverse_crit * inverse_crit
            parts.append((radius_sq, signal, weight))
        for edge in range(first_edge, len(edge_sq)):
            masks = [radius_sq < edge_sq[edge] for radius_sq, _, _ in parts]
            signal_sum = sum(jnp.where(m, part[1], 0.0) for m, part in zip(masks, parts))
            weight_sum = sum(jnp.where(m, part[2], 0.0) for m, part in zip(masks, parts))
            sums[edge, 0] += signal_sum
            sums[edge, 1] += weight_sum

    def tile_step(tile_index, carry):
        sums[...] = jnp.zeros_like(sums)

        def chunk_step(index, inner):
            chosen = class_ref[tile_index, index]
            for number, first_edge in enumerate(groups):
                @pl.when(chosen == number)
                def _():
                    visit(first_edge, tile_index, index // pieces, index % pieces)
            return inner

        lax.fori_loop(0, patches * pieces, chunk_step, 0)
        totals = jnp.sum(sums[...], axis=3)
        out_ref[tile_index] = jnp.concatenate(
            [totals[1:, 0] - totals[:-1, 0], totals[1:, 1] - totals[:-1, 1]], axis=0
        )
        return carry

    def guarded_step(tile_index, carry):
        @pl.when(class_ref[tile_index, patches * pieces] > 0)
        def _():
            tile_step(tile_index, 0)

        @pl.when(class_ref[tile_index, patches * pieces] <= 0)
        def _():
            out_ref[tile_index] = jnp.zeros(out_ref.shape[1:], jnp.float32)

        return carry

    lax.fori_loop(0, tiles, guarded_step, 0)


def on_device(lens_block, lens_count, lens_region, lens_sample, source_block):
    edge_sq = edge_squares()
    pdf_bins = source_block.shape[2] - 5
    width = source_block.shape[3]
    lens_total = lens_block.shape[3]
    tile = 32
    chunk = 256
    pieces = width // chunk
    groups = (0, 13, 17, 20)
    live_count = lens_count[0, 0]

    sources = source_block[0, 0]
    source_x = sources[pdf_bins].astype(jnp.int32)
    source_y = sources[pdf_bins + 1].astype(jnp.int32)
    source_rank = compact_order(source_x, source_y, jnp.zeros_like(source_x), width // 2)
    picked = (source_rank[:, None] == jnp.arange(width, dtype=jnp.int32)[None, :]).astype(jnp.bfloat16)
    sources = jnp.dot(sources, picked, preferred_element_type=jnp.float32).astype(jnp.bfloat16)
    partial_rows = extended(sources[None, None], (("ra", 0),), 1, True)
    beside_all = extended(partial_rows, (("dec", 1),), 1, False)
    beside_all = beside_all.reshape(9, sources.shape[0], width)

    lenses = lens_block[0, 0]
    slots = jnp.arange(lens_total, dtype=jnp.int32)
    dead = (slots >= live_count).astype(jnp.int32)
    lens_rank = compact_order(
        lenses[pdf_bins].astype(jnp.int32), lenses[pdf_bins + 1].astype(jnp.int32), dead, lens_total // 4
    )
    lens_hit = lens_rank[None, :] == slots[:, None]
    sorted_lenses = lax.dot_general(
        lens_hit.astype(jnp.bfloat16), lenses, (((1,), (1,)), ((), ())), preferred_element_type=jnp.float32
    )
    segment = lens_region[0, 0] * SAMPLES + lens_sample[0, 0]
    segment = jnp.sum(jnp.where(lens_hit, segment[None, :], 0), axis=1)
    lens_kernel = sorted_lenses[:, :pdf_bins].astype(jnp.bfloat16)
    lens_x = sorted_lenses[:, pdf_bins]
    lens_y = sorted_lenses[:, pdf_bins + 1]

    catalog = beside_all[:, pdf_bins:].astype(jnp.float32)
    shift = jnp.arange(9, dtype=jnp.int32)
    shift_x = ((shift // 3 - 1) * PATCH).astype(jnp.float32)[:, None]
    shift_y = ((shift % 3 - 1) * PATCH).astype(jnp.float32)[:, None]
    placed_x = catalog[:, 0] + shift_x
    placed_y = catalog[:, 1] + shift_y
    source_weight = catalog[:, 4]
    zero_row = jnp.zeros_like(placed_x)
    rows = jnp.stack(
        [
            placed_x,
            placed_y,
            -source_weight * catalog[:, 2],
            -2.0 * source_weight * catalog[:, 3],
            source_weight,
            zero_row,
            zero_row,
            zero_row,
        ],
        axis=1,
    )

    def gap(lens_at, source_at):
        lens_at = lens_at.reshape(-1, 1, tile)
        source_at = source_at.reshape(1, -1, chunk)
        apart = jnp.maximum(
            source_at.min(axis=2) - lens_at.max(axis=2), lens_at.min(axis=2) - source_at.max(axis=2)
        )
        return jnp.maximum(apart, 0.0)

    gap_x = gap(lens_x, placed_x)
    gap_y = gap(lens_y, placed_y)
    nearest_sq = gap_x * gap_x + gap_y * gap_y
    classes = sum((nearest_sq >= edge_sq[first - 1]).astype(jnp.int32) for first in groups[1:])
    classes = classes + (nearest_sq >= edge_sq[-1]).astype(jnp.int32)
    live_tile = (jnp.arange(lens_total // tile, dtype=jnp.int32) * tile < live_count).astype(jnp.int32)
    classes = jnp.concatenate([classes, live_tile[:, None]], axis=1)

    totals = pl.pallas_call(
        functools.partial(pair_kernel, edge_sq, groups, chunk),
        out_shape=jax.ShapeDtypeStruct((lens_total // tile, 2 * NBIN, tile), jnp.float32),
        in_specs=[pl.BlockSpec(memory_space=pltpu.SMEM)] + [pl.BlockSpec(memory_space=pltpu.VMEM)] * 5,
        out_specs=pl.BlockSpec(memory_space=pltpu.VMEM),
        scratch_shapes=[
            pltpu.VMEM((9, lens_total, width), jnp.float32),
            pltpu.VMEM((NBIN + 1, 2, tile, 128), jnp.float32),
        ],
        compiler_params=pltpu.CompilerParams(vmem_limit_bytes=48 * 2**20),
    )(
        classes,
        lens_kernel,
        jnp.broadcast_to(lens_x[:, None], (lens_total, 128)),
        jnp.broadcast_to(lens_y[:, None], (lens_total, 128)),
        beside_all[:, :pdf_bins],
        rows,
    )
    per_lens = jnp.transpose(totals, (0, 2, 1)).reshape(lens_total, 2 * NBIN)
    per_lens = jnp.where((slots < live_count)[:, None], per_lens, 0.0)
    devices = lax.axis_size("ra") * lax.axis_size("dec")
    region_table = jax.ops.segment_sum(per_lens, segment, num_segments=REG_DEV * devices * SAMPLES)
    region_table = region_table.reshape(devices, REG_DEV * SAMPLES * 2 * NBIN)
    received = lax.all_to_all(region_table, ("ra", "dec"), 0, 0, tiled=True)
    owned_rows = jnp.sum(received, axis=0).reshape(-1, SAMPLES, 2, NBIN)
    scales = bin_scales()
    return (owned_rows[:, :, 0, :] / jnp.sqrt(scales), owned_rows[:, :, 1, :] / scales)


def solution(mesh):
    placed = (
        P("ra", "dec", None, None),
        P("ra", "dec"),
        P("ra", "dec", None),
        P("ra", "dec", None),
        P("ra", "dec", None, None),
    )
    return jax.shard_map(
        on_device,
        mesh=mesh,
        in_specs=placed,
        out_specs=(P(("ra", "dec"), None, None), P(("ra", "dec"), None, None)),
        check_vma=False,
    )
```

time: 369 us -> 113 us (0.31)
  other arithmetic: 168 us -> 10.4 us
  waiting for transfers between devices: 152 us -> 11.6 us
  blocking collectives: 0 us -> 47.8 us
  Pallas kernels: 0 us -> 26.4 us
  matrix products: 18.2 us -> 3.08 us
  between operations: 14.9 us -> 1.6 us
    reduce_sum x8 -> x6, other arithmetic: 164 us -> 2 us  [the longest x4 1.62 us: ranks(): jnp.sum((unique[None, :] < unique[:, None]).astype(jnp.int32), axis=1)]
    unnamed x2 -> x0, waiting for transfers between devices: 139 us -> none
    all_to_all x0 -> x1, blocking collectives: none -> 47.8 us  [on_device(): received = lax.all_to_all(region_table, ('ra', 'dec'), 0, 0, tiled=True)]
    pallas_call x0 -> x1, Pallas kernels: none -> 26.4 us  [on_device(): pl.pallas_call(functools.partial(pair_kernel, edge_sq, groups, chunk), ou...]
    dot_general x36 -> x2, matrix products: 18.2 us -> 3.08 us  [the longest x1 1.82 us: on_device(): jnp.dot(sources, picked, preferred_element_type=jnp.float32)]
    ppermute x2, waiting for transfers between devices: 9.22 us -> 5.32 us  [extended(): lax.ppermute(lax.slice_in_dim(block, block.shape[dim] - width, None, axis...]
  transfers between devices with their start and end apart: 5 -> 4, of which waited for: 4 -> 4; matrix products, arithmetic and copies ran while one was open for 1% -> 3% of each run, Pallas kernels for 0% -> 0%
where the time goes in v1:
time: 113 us
  blocking collectives  47.8 us (42%)
  Pallas kernels  26.4 us (23%)
  waiting for transfers between devices  11.6 us (10%)
  other arithmetic  10.4 us (9%)
  starting transfers between devices  8.72 us (8%)
  local copies, waits for them, and re-layouts  3.17 us (3%)
  matrix products  3.08 us (3%)
  between operations  1.6 us (1%)
    all_to_all x1, blocking collectives, on_device(): received = lax.all_to_all(region_table, ('ra', 'dec'), 0, 0, tiled=True)  47.8 us
    pallas_call x1, Pallas kernels, on_device(): pl.pallas_call(functools.partial(pair_kernel, edge_sq, groups, chunk), ou...  26.4 us
    ppermute x2, waiting for transfers between devices, extended(): lax.ppermute(lax.slice_in_dim(block, 0, width, axis=dim), axis, backward)  6.24 us
    ppermute x2, waiting for transfers between devices, extended(): lax.ppermute(lax.slice_in_dim(block, block.shape[dim] - width, None, axis...  5.32 us
    ppermute x2, starting transfers between devices, extended(): lax.ppermute(lax.slice_in_dim(block, 0, width, axis=dim), axis, backward)  4.39 us
    ppermute x2, starting transfers between devices, extended(): lax.ppermute(lax.slice_in_dim(block, block.shape[dim] - width, None, axis...  4.32 us
    scatter-add x1, other arithmetic, on_device(): jax.ops.segment_sum(per_lens, segment, num_segments=REG_DEV * devices * S...  2.51 us
  transfers between devices with their start and end apart: 4, of which 4 were waited for; matrix products, arithmetic and copies ran while one was open for 3% of the time, Pallas kernels for 0%

profile of v1, /device:TPU:0, one launch (start us, length us, event | category | flops | bytes accessed | tf_op | source)
XLA Modules:
  0.0 112.7 jit_solution(17142739416490126156)
XLA Ops:
  0.6 0.7 convert_multiply_fusion
  1.4 0.7 slice_convert_fusion.2
  2.1 0.6 convert_reduce_fusion.1
  2.7 0.6 convert_reduce_fusion
  3.3 1.8 %fusion.3 = bf16[1,1,133,1024]{3,2,1,0:T(8,128)(2,1)S(1)} fusion(s32[1024]{0:T(1024)S(1)} %convert_reduce_fusion, bf16[1,1,133,1024]{3,2,1,0:T(8,128)(2,1)} %param.10), kind=kOutput, calls=%fused_computation.8 | convolution fusion | flops 280105984 | bytes 548864 | tf_op jit(solution)/shard_map/dot_general | solution.py:154
  5.1 3.0 %collective-permute-start = (bf16[1,1,133,1024]{3,2,1,0:T(8,128)(2,1)S(1)}, bf16[1,1,133,1024]{3,2,1,0:T(8,128)(2,1)S(1)}, u32[]{:S(2)}, u32[]{:S(2)}) collective-permute-start(bf16[1,1,133,1024]{3,2,1,0:T(8,128)(2,1)S(1)} %fusion.3), channel_id=1, source_target_pairs={{0,4},{4,8},{8,12},{12,16},{16,20},{20,24},{24,28},{28,0},{1,5},{5... | collective-permute-start | bytes 817160 | tf_op jit(solution)/shard_map/ppermute | solution.py:31
  8.1 3.1 %collective-permute-start.1 = (bf16[1,1,133,1024]{3,2,1,0:T(8,128)(2,1)S(1)}, bf16[1,1,133,1024]{3,2,1,0:T(8,128)(2,1)S(1)}, u32[]{:S(2)}, u32[]{:S(2)}) collective-permute-start(bf16[1,1,133,1024]{3,2,1,0:T(8,128)(2,1)S(1)} %fusion.3), channel_id=1, source_target_pairs={{4,0},{8,4},{12,8},{16,12},{20,16},{24,20},{28,24},{0,28},{5,1},{9... | collective-permute-start | bytes 817160 | tf_op jit(solution)/shard_map/ppermute | solution.py:34
  11.8 0.8 slice_convert_fusion.4
  12.6 0.2 convert_reduce_fusion.3
  12.9 0.3 convert_reduce_fusion.2
  13.5 1.3 %fusion.4 = f32[512,130]{0,1:T(8,128)S(1)} fusion(s32[512]{0:T(512)S(1)} %convert_reduce_fusion.2, bf16[1,1,130,512]{3,2,1,0:T(8,128)(2,1)} %param.6), kind=kOutput, calls=%fused_computation.11 | convolution fusion | flops 68419584 | bytes 401408 | tf_op jit(solution)/shard_map/dot_general | solution.py:166
  14.8 5.2 %collective-permute-done = bf16[1,1,133,1024]{3,2,1,0:T(8,128)(2,1)S(1)} collective-permute-done((bf16[1,1,133,1024]{3,2,1,0:T(8,128)(2,1)S(1)}, bf16[1,1,133,1024]{3,2,1,0:T(8,128)(2,1)S(1)}, u32[]{:S(2)}, u32[]{:S(2)}) %collective-permute-start) | collective-permute-done | bytes 272416 | tf_op jit(solution)/shard_map/ppermute | solution.py:31
  20.0 2.2 %collective-permute-done.1 = bf16[1,1,133,1024]{3,2,1,0:T(8,128)(2,1)S(1)} collective-permute-done((bf16[1,1,133,1024]{3,2,1,0:T(8,128)(2,1)S(1)}, bf16[1,1,133,1024]{3,2,1,0:T(8,128)(2,1)S(1)}, u32[]{:S(2)}, u32[]{:S(2)}) %collective-permute-start.1) | collective-permute-done | bytes 272416 | tf_op jit(solution)/shard_map/ppermute | solution.py:34
  22.2 1.0 pad_maximum_fusion.1
  23.2 1.3 %collective-permute-start.2 = (bf16[3,1,133,1024]{3,2,1,0:T(8,128)(2,1)}, bf16[3,1,133,1024]{3,2,1,0:T(8,128)(2,1)S(1)}, u32[]{:S(2)}, u32[]{:S(2)}) collective-permute-start(bf16[3,1,133,1024]{3,2,1,0:T(8,128)(2,1)} %pad_maximum_fusion.1), channel_id=1, source_target_pairs={{0,1},{1,2},{2,3},{4,5},{5,6},{6,7},{8,9},{9,10},{10,11},{12,13},{... | collective-permute-start | bytes 2451464 | tf_op jit(solution)/shard_map/ppermute | solution.py:31
  24.5 1.3 %collective-permute-start.3 = (bf16[3,1,133,1024]{3,2,1,0:T(8,128)(2,1)}, bf16[3,1,133,1024]{3,2,1,0:T(8,128)(2,1)S(1)}, u32[]{:S(2)}, u32[]{:S(2)}) collective-permute-start(bf16[3,1,133,1024]{3,2,1,0:T(8,128)(2,1)} %pad_maximum_fusion.1), channel_id=1, source_target_pairs={{1,0},{2,1},{3,2},{5,4},{6,5},{7,6},{9,8},{10,9},{11,10},{13,12},{... | collective-permute-start | bytes 2451464 | tf_op jit(solution)/shard_map/ppermute | solution.py:34
  26.3 0.2 select_reduce_fusion
  26.6 4.0 %collective-permute-done.3 = bf16[3,1,133,1024]{3,2,1,0:T(8,128)(2,1)S(1)} collective-permute-done((bf16[3,1,133,1024]{3,2,1,0:T(8,128)(2,1)}, bf16[3,1,133,1024]{3,2,1,0:T(8,128)(2,1)S(1)}, u32[]{:S(2)}, u32[]{:S(2)}) %collective-permute-start.3) | collective-permute-done | bytes 817184 | tf_op jit(solution)/shard_map/ppermute | solution.py:34
  30.7 0.3 pad_maximum_fusion
  31.0 0.2 slice.75.source_ref
  31.3 0.3 fusion.33
  31.7 0.2 add_reduce_fusion.3
  31.8 0.2 add_reduce_fusion.1
  32.2 0.5 stack.5.catalog_ref
  33.0 26.4 %shard_map.77 = f32[16,40,32]{2,1,0:T(8,128)S(1)} custom-call(s32[16,37]{1,0:T(8,128)S(1)} %pad_add_fusion.class_ref, bf16[512,128]{1,0:T(8,128)(2,1)S(1)} %copy.26.lens_ref, f32[512,128]{1,0:T(8,128)S(1)} %broadcast_in_dim.73.x_ref, f32[512,128]{1,0:T(8,128)S(1)} %broadcast_in_dim.75.y_ref, bf16[9,128,1024]{2,1,0:T(8,128)(2,1)S(1)} %slice.75.source_ref, ...), custom_call_target="tpu_custom_call" | custom-call | tf_op jit(solution)/shard_map/pallas_call | solution.py:213
  59.5 0.2 reshape.376
  59.8 2.5 %scatter_custom_fusion = f32[2048,40]{1,0:T(8,128)S(1)} fusion(s32[512]{0:T(512)S(1)} %select_reduce_fusion, f32[512,40]{1,0:T(8,128)S(1)} %copy.24, f32[]{:T(128)} %constant.36.clone.1), kind=kCustom, calls=%fused_computation.16 | custom fusion | flops 20480 | bytes 327684 | tf_op jit(solution)/shard_map/scatter-add | solution.py:234
  62.3 1.0 all_to_all.8
  63.3 47.8 %all_to_all.10 = f32[32,1,2560]{2,1,0:T(1,128)S(1)} all-to-all(f32[32,1,2560]{2,1,0:T(1,128)S(1)} %all_to_all.8), channel_id=1, replica_groups=mesh['ra'=8,'dec'=4] {'ra','dec'}, dimensions={0} | all-to-all | bytes 655360 | tf_op jit(solution)/shard_map/all_to_all | solution.py:236
  111.1 0.2 reduce_sum.59
  111.5 0.6 broadcast_multiply_fusion
  112.1 0.6 broadcast_multiply_fusion.1
  (41 shorter events, 1.9 us)
Async XLA Ops:
  1.4 24.9 %copy-start = (s32[1,1,512]{2,1,0:T(1,128)S(1)}, s32[1,1,512]{2,1,0:T(1,128)}, u32[]{:S(2)}) copy-start(s32[1,1,512]{2,1,0:T(1,128)} %param.9) | copy-start | bytes 6148
  1.4 24.9 %copy-start.1 = (s32[1,1,512]{2,1,0:T(1,128)S(1)}, s32[1,1,512]{2,1,0:T(1,128)}, u32[]{:S(2)}) copy-start(s32[1,1,512]{2,1,0:T(1,128)} %param.8) | copy-start | bytes 6148
  5.1 14.9 %collective-permute-start = (bf16[1,1,133,1024]{3,2,1,0:T(8,128)(2,1)S(1)}, bf16[1,1,133,1024]{3,2,1,0:T(8,128)(2,1)S(1)}, u32[]{:S(2)}, u32[]{:S(2)}) collective-permute-start(bf16[1,1,133,1024]{3,2,1,0:T(8,128)(2,1)S(1)} %fusion.3), channel_id=1, source_target_pairs={{0,4},{4,8},{8,12},{12,16},{16,20},{20,24},{24,28},{28,0},{1,5},{5... | collective-permute-start | bytes 817160 | tf_op jit(solution)/shard_map/ppermute | solution.py:31
  8.1 14.1 %collective-permute-start.1 = (bf16[1,1,133,1024]{3,2,1,0:T(8,128)(2,1)S(1)}, bf16[1,1,133,1024]{3,2,1,0:T(8,128)(2,1)S(1)}, u32[]{:S(2)}, u32[]{:S(2)}) collective-permute-start(bf16[1,1,133,1024]{3,2,1,0:T(8,128)(2,1)S(1)} %fusion.3), channel_id=1, source_target_pairs={{4,0},{8,4},{12,8},{16,12},{20,16},{24,20},{28,24},{0,28},{5,1},{9... | collective-permute-start | bytes 817160 | tf_op jit(solution)/shard_map/ppermute | solution.py:34
  23.2 3.5 %collective-permute-start.2 = (bf16[3,1,133,1024]{3,2,1,0:T(8,128)(2,1)}, bf16[3,1,133,1024]{3,2,1,0:T(8,128)(2,1)S(1)}, u32[]{:S(2)}, u32[]{:S(2)}) collective-permute-start(bf16[3,1,133,1024]{3,2,1,0:T(8,128)(2,1)} %pad_maximum_fusion.1), channel_id=1, source_target_pairs={{0,1},{1,2},{2,3},{4,5},{5,6},{6,7},{8,9},{9,10},{10,11},{12,13},{... | collective-permute-start | bytes 2451464 | tf_op jit(solution)/shard_map/ppermute | solution.py:31
  24.5 6.2 %collective-permute-start.3 = (bf16[3,1,133,1024]{3,2,1,0:T(8,128)(2,1)}, bf16[3,1,133,1024]{3,2,1,0:T(8,128)(2,1)S(1)}, u32[]{:S(2)}, u32[]{:S(2)}) collective-permute-start(bf16[3,1,133,1024]{3,2,1,0:T(8,128)(2,1)} %pad_maximum_fusion.1), channel_id=1, source_target_pairs={{1,0},{2,1},{3,2},{5,4},{6,5},{7,6},{9,8},{10,9},{11,10},{13,12},{... | collective-permute-start | bytes 2451464 | tf_op jit(solution)/shard_map/ppermute | solution.py:34
  59.4 52.1 %copy-start.3 = (f32[20]{0:T(128)S(1)}, f32[20]{0:T(128)}, u32[]{:S(2)}) copy-start(f32[20]{0:T(128)} %constant.92) | copy-start | bytes 244
  59.4 52.7 %copy-start.2 = (f32[20]{0:T(128)S(1)}, f32[20]{0:T(128)}, u32[]{:S(2)}) copy-start(f32[20]{0:T(128)} %constant.90) | copy-start | bytes 244

commit v2 on v1

--- a/solution.py
+++ b/solution.py
@@ -135,6 +135,83 @@
     lax.fori_loop(0, tiles, guarded_step, 0)
 
 
+def exchange_sum_kernel(table_ref, out_ref, first, partial, second, send_one, recv_one, send_two, recv_two):
+    me_ra, me_dec = lax.axis_index("ra"), lax.axis_index("dec")
+    count_ra, count_dec = lax.axis_size("ra"), lax.axis_size("dec")
+
+    def peer_ra(step):
+        return (lax.rem(me_ra + step, count_ra), me_dec)
+
+    def peer_dec(step):
+        return (me_ra, lax.rem(me_dec + step, count_dec))
+
+    mesh_ids = pl.DeviceIdType.MESH
+    barrier = pltpu.get_barrier_semaphore()
+    for step in range(1, count_dec):
+        pl.semaphore_signal(barrier, inc=1, device_id=peer_dec(step), device_id_type=mesh_ids)
+    for step in range(1, count_ra):
+        pl.semaphore_signal(barrier, inc=1, device_id=peer_ra(step), device_id_type=mesh_ids)
+    pl.semaphore_wait(barrier, count_dec + count_ra - 2)
+
+    copies = []
+    for step in range(1, count_dec):
+        copy = pltpu.make_async_remote_copy(
+            src_ref=table_ref.at[lax.rem(me_dec + step, count_dec)],
+            dst_ref=first.at[step - 1],
+            send_sem=send_one.at[step - 1],
+            recv_sem=recv_one.at[step - 1],
+            device_id=peer_dec(step),
+            device_id_type=mesh_ids,
+        )
+        copy.start()
+        copies.append(copy)
+    partial[...] = table_ref[me_dec]
+    for step in range(1, count_dec):
+        copies[step - 1].wait_recv()
+        partial[...] += first[step - 1]
+    late = []
+    for step in range(1, count_ra):
+        copy = pltpu.make_async_remote_copy(
+            src_ref=partial.at[lax.rem(me_ra + step, count_ra)],
+            dst_ref=second.at[step - 1],
+            send_sem=send_two.at[step - 1],
+            recv_sem=recv_two.at[step - 1],
+            device_id=peer_ra(step),
+            device_id_type=mesh_ids,
+        )
+        copy.start()
+        late.append(copy)
+    total = partial[me_ra]
+    for step in range(1, count_ra):
+        late[step - 1].wait_recv()
+        total = total + second[step - 1]
+    out_ref[...] = total
+    for copy in copies + late:
+        copy.wait_send()
+
+
+def exchange_sum(table):
+    count_dec, count_ra, rows, columns = table.shape
+    return pl.pallas_call(
+        exchange_sum_kernel,
+        out_shape=jax.ShapeDtypeStruct((rows, columns), jnp.float32),
+        in_specs=[pl.BlockSpec(memory_space=pltpu.VMEM)],
+        out_specs=pl.BlockSpec(memory_space=pltpu.VMEM),
+        scratch_shapes=[
+            pltpu.VMEM((count_dec - 1, count_ra, rows, columns), jnp.float32),
+            pltpu.VMEM((count_ra, rows, columns), jnp.float32),
+            pltpu.VMEM((count_ra - 1, rows, columns), jnp.float32),
+            pltpu.SemaphoreType.DMA((count_dec - 1,)),
+            pltpu.SemaphoreType.DMA((count_dec - 1,)),
+            pltpu.SemaphoreType.DMA((count_ra - 1,)),
+            pltpu.SemaphoreType.DMA((count_ra - 1,)),
+        ],
+        compiler_params=pltpu.CompilerParams(
+            collective_id=0, has_side_effects=True, vmem_limit_bytes=32 * 2**20
+        ),
+    )(table)
+
+
 def on_device(lens_block, lens_count, lens_region, lens_sample, source_block):
     edge_sq = edge_squares()
     pdf_bins = source_block.shape[2] - 5
@@ -166,7 +243,10 @@
     sorted_lenses = lax.dot_general(
         lens_hit.astype(jnp.bfloat16), lenses, (((1,), (1,)), ((), ())), preferred_element_type=jnp.float32
     )
-    segment = lens_region[0, 0] * SAMPLES + lens_sample[0, 0]
+    owner = lens_region[0, 0] // REG_DEV
+    count_dec = lax.axis_size("dec")
+    owner = owner % count_dec * lax.axis_size("ra") + owner // count_dec
+    segment = (owner * REG_DEV + lens_region[0, 0] % REG_DEV) * SAMPLES + lens_sample[0, 0]
     segment = jnp.sum(jnp.where(lens_hit, segment[None, :], 0), axis=1)
     lens_kernel = sorted_lenses[:, :pdf_bins].astype(jnp.bfloat16)
     lens_x = sorted_lenses[:, pdf_bins]
@@ -230,11 +310,10 @@
     )
     per_lens = jnp.transpose(totals, (0, 2, 1)).reshape(lens_total, 2 * NBIN)
     per_lens = jnp.where((slots < live_count)[:, None], per_lens, 0.0)
-    devices = lax.axis_size("ra") * lax.axis_size("dec")
-    region_table = jax.ops.segment_sum(per_lens, segment, num_segments=REG_DEV * devices * SAMPLES)
-    region_table = region_table.reshape(devices, REG_DEV * SAMPLES * 2 * NBIN)
-    received = lax.all_to_all(region_table, ("ra", "dec"), 0, 0, tiled=True)
-    owned_rows = jnp.sum(received, axis=0).reshape(-1, SAMPLES, 2, NBIN)
+    count_ra, count_dec = lax.axis_size("ra"), lax.axis_size("dec")
+    region_table = jax.ops.segment_sum(per_lens, segment, num_segments=REG_DEV * count_ra * count_dec * SAMPLES)
+    region_table = region_table.reshape(count_dec, count_ra, REG_DEV * SAMPLES * 2 * NBIN // 128, 128)
+    owned_rows = exchange_sum(region_table).reshape(-1, SAMPLES, 2, NBIN)
     scales = bin_scales()
     return (owned_rows[:, :, 0, :] / jnp.sqrt(scales), owned_rows[:, :, 1, :] / scales)
 

time: 113 us -> 108 us (0.956)
  blocking collectives: 47.8 us -> 0 us
  Pallas kernels: 26.4 us -> 69.9 us
    pallas_call x0 -> x1, Pallas kernels: none -> 52.7 us  [exchange_sum(): pl.pallas_call(exchange_sum_kernel, out_shape=jax.ShapeDtypeStruct((rows,...]
    all_to_all x1 -> x0, blocking collectives: 47.8 us -> none  [on_device(): received = lax.all_to_all(region_table, ('ra', 'dec'), 0, 0, tiled=True)]
    pallas_call x1, Pallas kernels: 26.4 us -> 17.2 us  [on_device(): pl.pallas_call(functools.partial(pair_kernel, edge_sq, groups, chunk), ou...]
where the time goes in v2:
time: 108 us
  Pallas kernels  69.9 us (65%)
  waiting for transfers between devices  11.5 us (11%)
  other arithmetic  10.2 us (9%)
  starting transfers between devices  8.71 us (8%)
  matrix products  3.09 us (3%)
  local copies, waits for them, and re-layouts  2.95 us (3%)
  between operations  1.59 us (1%)
    pallas_call x1, Pallas kernels, exchange_sum(): pl.pallas_call(exchange_sum_kernel, out_shape=jax.ShapeDtypeStruct((rows,...  52.7 us
    pallas_call x1, Pallas kernels, on_device(): pl.pallas_call(functools.partial(pair_kernel, edge_sq, groups, chunk), ou...  17.2 us
    ppermute x2, waiting for transfers between devices, extended(): lax.ppermute(lax.slice_in_dim(block, 0, width, axis=dim), axis, backward)  6.24 us
    ppermute x2, waiting for transfers between devices, extended(): lax.ppermute(lax.slice_in_dim(block, block.shape[dim] - width, None, axis...  5.3 us
    ppermute x2, starting transfers between devices, extended(): lax.ppermute(lax.slice_in_dim(block, 0, width, axis=dim), axis, backward)  4.39 us
    ppermute x2, starting transfers between devices, extended(): lax.ppermute(lax.slice_in_dim(block, block.shape[dim] - width, None, axis...  4.32 us
    scatter-add x1, other arithmetic, on_device(): jax.ops.segment_sum(per_lens, segment, num_segments=REG_DEV * count_ra *...  2.51 us
  transfers between devices with their start and end apart: 4, of which 4 were waited for; matrix products, arithmetic and copies ran while one was open for 3% of the time, Pallas kernels for 0%

profile of v2, /device:TPU:0, one launch (start us, length us, event | category | flops | bytes accessed | tf_op | source)
XLA Modules:
  0.0 108.0 jit_solution(16383751483941678070)
XLA Ops:
  0.6 0.7 convert_multiply_fusion
  1.4 0.7 slice_convert_fusion.2
  2.1 0.6 convert_reduce_fusion.1
  2.7 0.6 convert_reduce_fusion
  3.3 1.8 %fusion.3 = bf16[1,1,133,1024]{3,2,1,0:T(8,128)(2,1)S(1)} fusion(s32[1024]{0:T(1024)S(1)} %convert_reduce_fusion, bf16[1,1,133,1024]{3,2,1,0:T(8,128)(2,1)} %param.10), kind=kOutput, calls=%fused_computation.8 | convolution fusion | flops 280105984 | bytes 548864 | tf_op jit(solution)/shard_map/dot_general | solution.py:231
  5.1 3.0 %collective-permute-start = (bf16[1,1,133,1024]{3,2,1,0:T(8,128)(2,1)S(1)}, bf16[1,1,133,1024]{3,2,1,0:T(8,128)(2,1)S(1)}, u32[]{:S(2)}, u32[]{:S(2)}) collective-permute-start(bf16[1,1,133,1024]{3,2,1,0:T(8,128)(2,1)S(1)} %fusion.3), channel_id=1, source_target_pairs={{0,4},{4,8},{8,12},{12,16},{16,20},{20,24},{24,28},{28,0},{1,5},{5... | collective-permute-start | bytes 817160 | tf_op jit(solution)/shard_map/ppermute | solution.py:31
  8.1 3.1 %collective-permute-start.1 = (bf16[1,1,133,1024]{3,2,1,0:T(8,128)(2,1)S(1)}, bf16[1,1,133,1024]{3,2,1,0:T(8,128)(2,1)S(1)}, u32[]{:S(2)}, u32[]{:S(2)}) collective-permute-start(bf16[1,1,133,1024]{3,2,1,0:T(8,128)(2,1)S(1)} %fusion.3), channel_id=1, source_target_pairs={{4,0},{8,4},{12,8},{16,12},{20,16},{24,20},{28,24},{0,28},{5,1},{9... | collective-permute-start | bytes 817160 | tf_op jit(solution)/shard_map/ppermute | solution.py:34
  11.8 0.8 slice_convert_fusion.4
  12.6 0.2 convert_reduce_fusion.3
  12.9 0.3 convert_reduce_fusion.2
  13.5 1.3 %fusion.4 = f32[512,130]{0,1:T(8,128)S(1)} fusion(s32[512]{0:T(512)S(1)} %convert_reduce_fusion.2, bf16[1,1,130,512]{3,2,1,0:T(8,128)(2,1)} %param.6), kind=kOutput, calls=%fused_computation.11 | convolution fusion | flops 68419584 | bytes 401408 | tf_op jit(solution)/shard_map/dot_general | solution.py:243
  14.8 5.2 %collective-permute-done = bf16[1,1,133,1024]{3,2,1,0:T(8,128)(2,1)S(1)} collective-permute-done((bf16[1,1,133,1024]{3,2,1,0:T(8,128)(2,1)S(1)}, bf16[1,1,133,1024]{3,2,1,0:T(8,128)(2,1)S(1)}, u32[]{:S(2)}, u32[]{:S(2)}) %collective-permute-start) | collective-permute-done | bytes 272416 | tf_op jit(solution)/shard_map/ppermute | solution.py:31
  20.0 2.2 %collective-permute-done.1 = bf16[1,1,133,1024]{3,2,1,0:T(8,128)(2,1)S(1)} collective-permute-done((bf16[1,1,133,1024]{3,2,1,0:T(8,128)(2,1)S(1)}, bf16[1,1,133,1024]{3,2,1,0:T(8,128)(2,1)S(1)}, u32[]{:S(2)}, u32[]{:S(2)}) %collective-permute-start.1) | collective-permute-done | bytes 272416 | tf_op jit(solution)/shard_map/ppermute | solution.py:34
  22.2 1.0 pad_maximum_fusion.1
  23.2 1.3 %collective-permute-start.2 = (bf16[3,1,133,1024]{3,2,1,0:T(8,128)(2,1)}, bf16[3,1,133,1024]{3,2,1,0:T(8,128)(2,1)S(1)}, u32[]{:S(2)}, u32[]{:S(2)}) collective-permute-start(bf16[3,1,133,1024]{3,2,1,0:T(8,128)(2,1)} %pad_maximum_fusion.1), channel_id=1, source_target_pairs={{0,1},{1,2},{2,3},{4,5},{5,6},{6,7},{8,9},{9,10},{10,11},{12,13},{... | collective-permute-start | bytes 2451464 | tf_op jit(solution)/shard_map/ppermute | solution.py:31
  24.5 1.3 %collective-permute-start.3 = (bf16[3,1,133,1024]{3,2,1,0:T(8,128)(2,1)}, bf16[3,1,133,1024]{3,2,1,0:T(8,128)(2,1)S(1)}, u32[]{:S(2)}, u32[]{:S(2)}) collective-permute-start(bf16[3,1,133,1024]{3,2,1,0:T(8,128)(2,1)} %pad_maximum_fusion.1), channel_id=1, source_target_pairs={{1,0},{2,1},{3,2},{5,4},{6,5},{7,6},{9,8},{10,9},{11,10},{13,12},{... | collective-permute-start | bytes 2451464 | tf_op jit(solution)/shard_map/ppermute | solution.py:34
  26.1 0.1 fusion.40
  26.3 0.2 select_reduce_fusion
  26.6 4.0 %collective-permute-done.3 = bf16[3,1,133,1024]{3,2,1,0:T(8,128)(2,1)S(1)} collective-permute-done((bf16[3,1,133,1024]{3,2,1,0:T(8,128)(2,1)}, bf16[3,1,133,1024]{3,2,1,0:T(8,128)(2,1)S(1)}, u32[]{:S(2)}, u32[]{:S(2)}) %collective-permute-start.3) | collective-permute-done | bytes 817184 | tf_op jit(solution)/shard_map/ppermute | solution.py:34
  30.7 0.3 pad_maximum_fusion
  31.0 0.2 slice.75.source_ref
  31.3 0.3 fusion.42
  31.7 0.2 add_reduce_fusion.3
  31.8 0.2 add_reduce_fusion.1
  32.2 0.5 stack.5.catalog_ref
  33.0 17.2 %shard_map.77 = f32[16,40,32]{2,1,0:T(8,128)S(1)} custom-call(s32[16,37]{1,0:T(8,128)S(1)} %pad_add_fusion.class_ref, bf16[512,128]{1,0:T(8,128)(2,1)S(1)} %copy.30.lens_ref, f32[512,128]{1,0:T(8,128)S(1)} %broadcast_in_dim.73.x_ref, f32[512,128]{1,0:T(8,128)S(1)} %broadcast_in_dim.75.y_ref, bf16[9,128,1024]{2,1,0:T(8,128)(2,1)S(1)} %slice.75.source_ref, ...), custom_call_target="tpu_custom_call" | custom-call | tf_op jit(solution)/shard_map/pallas_call | solution.py:293
  50.3 0.2 reshape.446
  50.6 2.5 %scatter_custom_fusion = f32[2048,40]{1,0:T(8,128)S(1)} fusion(s32[512]{0:T(512)S(1)} %select_reduce_fusion, f32[512,40]{1,0:T(8,128)S(1)} %copy.27, f32[]{:T(128)} %constant.100.clone.1), kind=kCustom, calls=%fused_computation.16 | custom fusion | flops 20480 | bytes 327684 | tf_op jit(solution)/shard_map/scatter-add | solution.py:314
  53.1 0.7 reshape.447.table_ref
  53.9 52.7 %shard_map.78 = f32[20,128]{1,0:T(8,128)S(1)} custom-call(f32[4,8,20,128]{3,2,1,0:T(8,128)S(1)} %reshape.447.table_ref), custom_call_target="tpu_custom_call" | custom-call | tf_op jit(solution)/shard_map/pallas_call | solution.py:195
  106.8 0.6 broadcast_multiply_fusion
  107.4 0.6 broadcast_multiply_fusion.1
  (40 shorter events, 1.7 us)
Async XLA Ops:
  2.1 24.2 %copy-start = (s32[1,1,512]{2,1,0:T(1,128)S(1)}, s32[1,1,512]{2,1,0:T(1,128)}, u32[]{:S(2)}) copy-start(s32[1,1,512]{2,1,0:T(1,128)} %param.9) | copy-start | bytes 6148
  2.1 24.2 %copy-start.1 = (s32[1,1,512]{2,1,0:T(1,128)S(1)}, s32[1,1,512]{2,1,0:T(1,128)}, u32[]{:S(2)}) copy-start(s32[1,1,512]{2,1,0:T(1,128)} %param.8) | copy-start | bytes 6148
  5.1 14.9 %collective-permute-start = (bf16[1,1,133,1024]{3,2,1,0:T(8,128)(2,1)S(1)}, bf16[1,1,133,1024]{3,2,1,0:T(8,128)(2,1)S(1)}, u32[]{:S(2)}, u32[]{:S(2)}) collective-permute-start(bf16[1,1,133,1024]{3,2,1,0:T(8,128)(2,1)S(1)} %fusion.3), channel_id=1, source_target_pairs={{0,4},{4,8},{8,12},{12,16},{16,20},{20,24},{24,28},{28,0},{1,5},{5... | collective-permute-start | bytes 817160 | tf_op jit(solution)/shard_map/ppermute | solution.py:31
  8.1 14.1 %collective-permute-start.1 = (bf16[1,1,133,1024]{3,2,1,0:T(8,128)(2,1)S(1)}, bf16[1,1,133,1024]{3,2,1,0:T(8,128)(2,1)S(1)}, u32[]{:S(2)}, u32[]{:S(2)}) collective-permute-start(bf16[1,1,133,1024]{3,2,1,0:T(8,128)(2,1)S(1)} %fusion.3), channel_id=1, source_target_pairs={{4,0},{8,4},{12,8},{16,12},{20,16},{24,20},{28,24},{0,28},{5,1},{9... | collective-permute-start | bytes 817160 | tf_op jit(solution)/shard_map/ppermute | solution.py:34
  23.2 3.5 %collective-permute-start.2 = (bf16[3,1,133,1024]{3,2,1,0:T(8,128)(2,1)}, bf16[3,1,133,1024]{3,2,1,0:T(8,128)(2,1)S(1)}, u32[]{:S(2)}, u32[]{:S(2)}) collective-permute-start(bf16[3,1,133,1024]{3,2,1,0:T(8,128)(2,1)} %pad_maximum_fusion.1), channel_id=1, source_target_pairs={{0,1},{1,2},{2,3},{4,5},{5,6},{6,7},{8,9},{9,10},{10,11},{12,13},{... | collective-permute-start | bytes 2451464 | tf_op jit(solution)/shard_map/ppermute | solution.py:31
  24.5 6.2 %collective-permute-start.3 = (bf16[3,1,133,1024]{3,2,1,0:T(8,128)(2,1)}, bf16[3,1,133,1024]{3,2,1,0:T(8,128)(2,1)S(1)}, u32[]{:S(2)}, u32[]{:S(2)}) collective-permute-start(bf16[3,1,133,1024]{3,2,1,0:T(8,128)(2,1)} %pad_maximum_fusion.1), channel_id=1, source_target_pairs={{1,0},{2,1},{3,2},{5,4},{6,5},{7,6},{9,8},{10,9},{11,10},{13,12},{... | collective-permute-start | bytes 2451464 | tf_op jit(solution)/shard_map/ppermute | solution.py:34
  50.2 56.6 %copy-start.3 = (f32[20]{0:T(128)S(1)}, f32[20]{0:T(128)}, u32[]{:S(2)}) copy-start(f32[20]{0:T(128)} %constant.131) | copy-start | bytes 244
  50.2 57.2 %copy-start.2 = (f32[20]{0:T(128)S(1)}, f32[20]{0:T(128)}, u32[]{:S(2)}) copy-start(f32[20]{0:T(128)} %constant.129) | copy-start | bytes 244

commit v3 on v2

--- a/solution.py
+++ b/solution.py
@@ -65,45 +65,40 @@
     return ranks(strip * (4 * PATCH) + position_y + 2 * PATCH * dead)
 
 
-def pair_kernel(edge_sq, groups, chunk, class_ref, lens_ref, x_ref, y_ref, source_ref, catalog_ref, out_ref, crit, sums):
+def pair_kernel(edge_sq, groups, chunk, class_ref, lens_ref, place_ref, source_ref, catalog_ref, out_ref, crit, sums):
     patches, _, width = source_ref.shape
-    tile = out_ref.shape[2]
-    tiles = out_ref.shape[0]
+    tiles, _, tile = out_ref.shape
     pieces = width // chunk
 
     def crit_step(patch, carry):
-        crit[patch] = jnp.dot(lens_ref[...], source_ref[patch], preferred_element_type=jnp.float32)
+        crit[patch] = lax.dot_general(
+            source_ref[patch], lens_ref[...], (((0,), (0,)), ((), ())), preferred_element_type=jnp.float32
+        )
         return carry
 
     lax.fori_loop(0, patches, crit_step, 0)
 
     def visit(first_edge, tile_index, patch, piece):
-        rows = pl.ds(pl.multiple_of(tile_index * tile, tile), tile)
-        lens_x = x_ref[rows, :]
-        lens_y = y_ref[rows, :]
-        parts = []
-        for part in range(chunk // 128):
-            columns = pl.ds(pl.multiple_of(piece * chunk + part * 128, 128), 128)
-            inverse_crit = crit[patch, rows, columns]
-            catalog = catalog_ref[patch, :, columns]
-            delta_x = catalog[0:1] - lens_x
-            delta_y = catalog[1:2] - lens_y
-            square_x = delta_x * delta_x
-            square_y = delta_y * delta_y
-            radius_sq = square_x + square_y
-            inverse = 1.0 / jnp.maximum(radius_sq, edge_sq[0])
-            turned = catalog[2:3] * (square_x - square_y) + catalog[3:4] * (delta_x * delta_y)
-            signal = inverse_crit * (turned * inverse)
-            weight = catalog[4:5] * inverse_crit * inverse_crit
-            parts.append((radius_sq, signal, weight))
+        columns = pl.ds(pl.multiple_of(tile_index * tile, tile), tile)
+        rows = pl.ds(pl.multiple_of(piece * chunk, chunk), chunk)
+        inverse_crit = crit[patch, rows, columns]
+        catalog = catalog_ref[patch, rows, :]
+        delta_x = catalog[:, 0:1] - place_ref[0:1, columns]
+        delta_y = catalog[:, 1:2] - place_ref[1:2, columns]
+        square_x = delta_x * delta_x
+        square_y = delta_y * delta_y
+        radius_sq = square_x + square_y
+        inverse = 1.0 / jnp.maximum(radius_sq, edge_sq[0])
+        turned = catalog[:, 2:3] * (square_x - square_y) + catalog[:, 3:4] * (delta_x * delta_y)
+        signal = inverse_crit * (turned * inverse)
+        weight = catalog[:, 4:5] * inverse_crit * inverse_crit
         for edge in range(first_edge, len(edge_sq)):
-            masks = [radius_sq < edge_sq[edge] for radius_sq, _, _ in parts]
-            signal_sum = sum(jnp.where(m, part[1], 0.0) for m, part in zip(masks, parts))
-            weight_sum = sum(jnp.where(m, part[2], 0.0) for m, part in zip(masks, parts))
-            sums[edge, 0] += signal_sum
-            sums[edge, 1] += weight_sum
-
-    def tile_step(tile_index, carry):
+            inside = radius_sq < edge_sq[edge]
+            for number, values in enumerate((signal, weight)):
+                kept = jnp.where(inside, values, 0.0).reshape(chunk // 8, 8, tile)
+                sums[edge, number] += jnp.sum(kept, axis=0)
+
+    def tile_step(tile_index):
         sums[...] = jnp.zeros_like(sums)
 
         def chunk_step(index, inner):
@@ -115,16 +110,15 @@
             return inner
 
         lax.fori_loop(0, patches * pieces, chunk_step, 0)
-        totals = jnp.sum(sums[...], axis=3)
+        totals = jnp.sum(sums[...], axis=2)
         out_ref[tile_index] = jnp.concatenate(
             [totals[1:, 0] - totals[:-1, 0], totals[1:, 1] - totals[:-1, 1]], axis=0
         )
-        return carry
 
     def guarded_step(tile_index, carry):
         @pl.when(class_ref[tile_index, patches * pieces] > 0)
         def _():
-            tile_step(tile_index, 0)
+            tile_step(tile_index)
 
         @pl.when(class_ref[tile_index, patches * pieces] <= 0)
         def _():
@@ -217,16 +211,15 @@
     pdf_bins = source_block.shape[2] - 5
     width = source_block.shape[3]
     lens_total = lens_block.shape[3]
-    tile = 32
-    chunk = 256
-    pieces = width // chunk
-    groups = (0, 13, 17, 20)
+    tile = 128
+    chunk = 64
+    groups = (0, 8, 12, 14, 17, 18, 20)
     live_count = lens_count[0, 0]
 
     sources = source_block[0, 0]
     source_x = sources[pdf_bins].astype(jnp.int32)
     source_y = sources[pdf_bins + 1].astype(jnp.int32)
-    source_rank = compact_order(source_x, source_y, jnp.zeros_like(source_x), width // 2)
+    source_rank = compact_order(source_x, source_y, jnp.zeros_like(source_x), width // 4)
     picked = (source_rank[:, None] == jnp.arange(width, dtype=jnp.int32)[None, :]).astype(jnp.bfloat16)
     sources = jnp.dot(sources, picked, preferred_element_type=jnp.float32).astype(jnp.bfloat16)
     partial_rows = extended(sources[None, None], (("ra", 0),), 1, True)
@@ -237,20 +230,20 @@
     slots = jnp.arange(lens_total, dtype=jnp.int32)
     dead = (slots >= live_count).astype(jnp.int32)
     lens_rank = compact_order(
-        lenses[pdf_bins].astype(jnp.int32), lenses[pdf_bins + 1].astype(jnp.int32), dead, lens_total // 4
+        lenses[pdf_bins].astype(jnp.int32), lenses[pdf_bins + 1].astype(jnp.int32), dead, lens_total // 2
     )
     lens_hit = lens_rank[None, :] == slots[:, None]
     sorted_lenses = lax.dot_general(
-        lens_hit.astype(jnp.bfloat16), lenses, (((1,), (1,)), ((), ())), preferred_element_type=jnp.float32
+        lenses, lens_hit.astype(jnp.bfloat16), (((1,), (1,)), ((), ())), preferred_element_type=jnp.float32
     )
     owner = lens_region[0, 0] // REG_DEV
     count_dec = lax.axis_size("dec")
     owner = owner % count_dec * lax.axis_size("ra") + owner // count_dec
     segment = (owner * REG_DEV + lens_region[0, 0] % REG_DEV) * SAMPLES + lens_sample[0, 0]
     segment = jnp.sum(jnp.where(lens_hit, segment[None, :], 0), axis=1)
-    lens_kernel = sorted_lenses[:, :pdf_bins].astype(jnp.bfloat16)
-    lens_x = sorted_lenses[:, pdf_bins]
-    lens_y = sorted_lenses[:, pdf_bins + 1]
+    lens_kernel = sorted_lenses[:pdf_bins].astype(jnp.bfloat16)
+    lens_places = sorted_lenses[pdf_bins:]
+    lens_x, lens_y = lens_places[0], lens_places[1]
 
     catalog = beside_all[:, pdf_bins:].astype(jnp.float32)
     shift = jnp.arange(9, dtype=jnp.int32)
@@ -271,7 +264,7 @@
             zero_row,
             zero_row,
         ],
-        axis=1,
+        axis=2,
     )
 
     def gap(lens_at, source_at):
@@ -293,18 +286,17 @@
     totals = pl.pallas_call(
         functools.partial(pair_kernel, edge_sq, groups, chunk),
         out_shape=jax.ShapeDtypeStruct((lens_total // tile, 2 * NBIN, tile), jnp.float32),
-        in_specs=[pl.BlockSpec(memory_space=pltpu.SMEM)] + [pl.BlockSpec(memory_space=pltpu.VMEM)] * 5,
+        in_specs=[pl.BlockSpec(memory_space=pltpu.SMEM)] + [pl.BlockSpec(memory_space=pltpu.VMEM)] * 4,
         out_specs=pl.BlockSpec(memory_space=pltpu.VMEM),
         scratch_shapes=[
-            pltpu.VMEM((9, lens_total, width), jnp.float32),
-            pltpu.VMEM((NBIN + 1, 2, tile, 128), jnp.float32),
+            pltpu.VMEM((9, width, lens_total), jnp.float32),
+            pltpu.VMEM((NBIN + 1, 2, 8, tile), jnp.float32),
         ],
         compiler_params=pltpu.CompilerParams(vmem_limit_bytes=48 * 2**20),
     )(
         classes,
         lens_kernel,
-        jnp.broadcast_to(lens_x[:, None], (lens_total, 128)),
-        jnp.broadcast_to(lens_y[:, None], (lens_total, 128)),
+        lens_places,
         beside_all[:, :pdf_bins],
         rows,
     )

time: 108 us -> 138 us (1.28)
  Pallas kernels: 69.9 us -> 99.1 us
  waiting for transfers between devices: 11.5 us -> 8.91 us
  local copies, waits for them, and re-layouts: 2.95 us -> 5.38 us
  starting transfers between devices: 8.71 us -> 10.4 us
    pallas_call x1, Pallas kernels: 52.7 us -> 73.2 us  [exchange_sum(): pl.pallas_call(exchange_sum_kernel, out_shape=jax.ShapeDtypeStruct((rows,...]
    pallas_call x1, Pallas kernels: 17.2 us -> 25.9 us  [on_device(): pl.pallas_call(functools.partial(pair_kernel, edge_sq, groups, chunk), ou...]
    ppermute x2, waiting for transfers between devices: 6.24 us -> 2.65 us  [extended(): lax.ppermute(lax.slice_in_dim(block, 0, width, axis=dim), axis, backward)]
    ppermute x2, starting transfers between devices: 4.39 us -> 7.31 us  [extended(): lax.ppermute(lax.slice_in_dim(block, 0, width, axis=dim), axis, backward)]
    another operation x3 -> x4, local copies, waits for them, and re-layouts: 0.51 us -> 3.37 us  [on_device(): jnp.stack([placed_x, placed_y, -source_weight * catalog[:, 2], -2.0 * sou...]
  transfers between devices with their start and end apart: 4 -> 4, of which waited for: 4 -> 3; matrix products, arithmetic and copies ran while one was open for 3% -> 2% of each run, Pallas kernels for 0% -> 0%
where the time goes in v3:
time: 138 us; the launch traced here: 139 us
  Pallas kernels  99.1 us (72%)
  starting transfers between devices  10.4 us (8%)
  other arithmetic  10.1 us (7%)
  waiting for transfers between devices  8.91 us (6%)
  local copies, waits for them, and re-layouts  5.38 us (4%)
  matrix products  3.08 us (2%)
  between operations  1.57 us (1%)
    pallas_call x1, Pallas kernels, exchange_sum(): pl.pallas_call(exchange_sum_kernel, out_shape=jax.ShapeDtypeStruct((rows,...  73.2 us
    pallas_call x1, Pallas kernels, on_device(): pl.pallas_call(functools.partial(pair_kernel, edge_sq, groups, chunk), ou...  25.9 us
    ppermute x2, starting transfers between devices, extended(): lax.ppermute(lax.slice_in_dim(block, 0, width, axis=dim), axis, backward)  7.31 us
    ppermute x2, waiting for transfers between devices, extended(): lax.ppermute(lax.slice_in_dim(block, block.shape[dim] - width, None, axis...  6.26 us
    another operation x4, local copies, waits for them, and re-layouts, on_device(): jnp.stack([placed_x, placed_y, -source_weight * catalog[:, 2], -2.0 * sou...  3.37 us
    ppermute x2, starting transfers between devices, extended(): lax.ppermute(lax.slice_in_dim(block, block.shape[dim] - width, None, axis...  3.08 us
  transfers between devices with their start and end apart: 4, of which 3 were waited for; matrix products, arithmetic and copies ran while one was open for 2% of the time, Pallas kernels for 0%

profile of v3, /device:TPU:0, one launch (start us, length us, event | category | flops | bytes accessed | tf_op | source)
XLA Modules:
  0.0 138.5 jit_solution(2250921578954173528)
XLA Ops:
  0.6 0.7 convert_multiply_fusion
  1.4 0.7 slice_convert_fusion.2
  2.1 0.6 convert_reduce_fusion.1
  2.7 0.6 convert_reduce_fusion
  3.3 1.8 %fusion.3 = bf16[1,1,133,1024]{3,2,1,0:T(8,128)(2,1)S(1)} fusion(s32[1024]{0:T(1024)S(1)} %convert_reduce_fusion, bf16[1,1,133,1024]{3,2,1,0:T(8,128)(2,1)} %param.10), kind=kOutput, calls=%fused_computation.9 | convolution fusion | flops 280105984 | bytes 548864 | tf_op jit(solution)/shard_map/dot_general | solution.py:224
  5.1 6.0 %collective-permute-start.1 = (bf16[1,1,133,1024]{3,2,1,0:T(8,128)(2,1)S(1)}, bf16[1,1,133,1024]{3,2,1,0:T(8,128)(2,1)S(1)}, u32[]{:S(2)}, u32[]{:S(2)}) collective-permute-start(bf16[1,1,133,1024]{3,2,1,0:T(8,128)(2,1)S(1)} %fusion.3), channel_id=1, source_target_pairs={{4,0},{8,4},{12,8},{16,12},{20,16},{24,20},{28,24},{0,28},{5,1},{9... | collective-permute-start | bytes 817160 | tf_op jit(solution)/shard_map/ppermute | solution.py:34
  11.8 0.8 slice_convert_fusion.4
  12.6 0.2 convert_reduce_fusion.3
  12.9 0.3 convert_reduce_fusion.2
  13.1 1.3 convolution_bitcast_fusion
  14.4 2.7 %collective-permute-done.1 = bf16[1,1,133,1024]{3,2,1,0:T(8,128)(2,1)S(1)} collective-permute-done((bf16[1,1,133,1024]{3,2,1,0:T(8,128)(2,1)S(1)}, bf16[1,1,133,1024]{3,2,1,0:T(8,128)(2,1)S(1)}, u32[]{:S(2)}, u32[]{:S(2)}) %collective-permute-start.1) | collective-permute-done | bytes 272416 | tf_op jit(solution)/shard_map/ppermute | solution.py:34
  17.0 4.9 %collective-permute-done = bf16[1,1,133,1024]{3,2,1,0:T(8,128)(2,1)S(1)} collective-permute-done((bf16[1,1,133,1024]{3,2,1,0:T(8,128)(2,1)S(1)}, bf16[1,1,133,1024]{3,2,1,0:T(8,128)(2,1)S(1)}, u32[]{:S(2)}, u32[]{:S(2)}) %collective-permute-start) | collective-permute-done | bytes 272416 | tf_op jit(solution)/shard_map/ppermute | solution.py:31
  21.9 1.0 pad_maximum_fusion.1
  22.9 1.3 collective-permute-start.3
  24.2 3.1 %collective-permute-start.2 = (bf16[3,1,133,1024]{3,2,1,0:T(8,128)(2,1)}, bf16[3,1,133,1024]{3,2,1,0:T(8,128)(2,1)S(1)}, u32[]{:S(2)}, u32[]{:S(2)}) collective-permute-start(bf16[3,1,133,1024]{3,2,1,0:T(8,128)(2,1)} %pad_maximum_fusion.1), channel_id=1, source_target_pairs={{0,1},{1,2},{2,3},{4,5},{5,6},{6,7},{8,9},{9,10},{10,11},{12,13},{... | collective-permute-start | bytes 2451464 | tf_op jit(solution)/shard_map/ppermute | solution.py:31
  27.7 0.1 fusion.41
  27.9 0.2 select_reduce_fusion
  28.1 1.4 collective-permute-done.2
  29.4 0.3 pad_maximum_fusion
  29.8 0.2 slice.82.source_ref
  30.0 0.2 fusion.9
  30.2 0.2 slice_reduce_fusion.1
  30.7 0.5 stack.5
  31.1 2.9 %copy.64.catalog_ref = f32[9,1024,8]{2,1,0:T(8,128)} copy(f32[9,1024,8]{1,2,0:T(8,128)S(1)} %stack.5) | data formatting | bytes 589824 | tf_op jit(solution)/shard_map/stack | solution.py:256
  34.0 0.3 add_reduce_fusion.1
  34.5 25.9 %shard_map.77 = f32[4,40,128]{2,1,0:T(8,128)S(1)} custom-call(s32[4,145]{1,0:T(4,128)S(1)} %pad_add_fusion.class_ref, bf16[128,512]{1,0:T(8,128)(2,1)S(1)} %slice.109.lens_ref, f32[2,512]{1,0:T(2,128)S(1)} %slice.81.place_ref, bf16[9,128,1024]{2,1,0:T(8,128)(2,1)S(1)} %slice.82.source_ref, f32[9,1024,8]{2,1,0:T(8,128)} %copy.64.catalog_ref), custom_call_target="tpu_custom_call" | custom-call | tf_op jit(solution)/shard_map/pallas_call | solution.py:286
  60.6 2.5 %scatter_custom_fusion = f32[2048,40]{1,0:T(8,128)S(1)} fusion(s32[512]{0:T(512)S(1)} %select_reduce_fusion, f32[512,40]{1,0:T(8,128)S(1)} %copy.66, f32[]{:T(128)} %constant.101.clone.1), kind=kCustom, calls=%fused_computation.16 | custom fusion | flops 20480 | bytes 327684 | tf_op jit(solution)/shard_map/scatter-add | solution.py:306
  63.1 0.7 reshape.537.table_ref
  63.9 73.2 %shard_map.78 = f32[20,128]{1,0:T(8,128)S(1)} custom-call(f32[4,8,20,128]{3,2,1,0:T(8,128)S(1)} %reshape.537.table_ref), custom_call_target="tpu_custom_call" | custom-call | tf_op jit(solution)/shard_map/pallas_call | solution.py:189
  137.1 0.1 reshape.538
  137.3 0.6 broadcast_multiply_fusion.1
  137.9 0.6 broadcast_multiply_fusion
  (36 shorter events, 1.0 us)
Async XLA Ops:
  0.6 27.2 %copy-start = (s32[1,1,512]{2,1,0:T(1,128)S(1)}, s32[1,1,512]{2,1,0:T(1,128)}, u32[]{:S(2)}) copy-start(s32[1,1,512]{2,1,0:T(1,128)} %param.9) | copy-start | bytes 6148
  0.6 27.2 %copy-start.1 = (s32[1,1,512]{2,1,0:T(1,128)S(1)}, s32[1,1,512]{2,1,0:T(1,128)}, u32[]{:S(2)}) copy-start(s32[1,1,512]{2,1,0:T(1,128)} %param.8) | copy-start | bytes 6148
  5.1 11.9 %collective-permute-start.1 = (bf16[1,1,133,1024]{3,2,1,0:T(8,128)(2,1)S(1)}, bf16[1,1,133,1024]{3,2,1,0:T(8,128)(2,1)S(1)}, u32[]{:S(2)}, u32[]{:S(2)}) collective-permute-start(bf16[1,1,133,1024]{3,2,1,0:T(8,128)(2,1)S(1)} %fusion.3), channel_id=1, source_target_pairs={{4,0},{8,4},{12,8},{16,12},{20,16},{24,20},{28,24},{0,28},{5,1},{9... | collective-permute-start | bytes 817160 | tf_op jit(solution)/shard_map/ppermute | solution.py:34
  11.1 10.8 %collective-permute-start = (bf16[1,1,133,1024]{3,2,1,0:T(8,128)(2,1)S(1)}, bf16[1,1,133,1024]{3,2,1,0:T(8,128)(2,1)S(1)}, u32[]{:S(2)}, u32[]{:S(2)}) collective-permute-start(bf16[1,1,133,1024]{3,2,1,0:T(8,128)(2,1)S(1)} %fusion.3), channel_id=1, source_target_pairs={{0,4},{4,8},{8,12},{12,16},{16,20},{20,24},{24,28},{28,0},{1,5},{5... | collective-permute-start | bytes 817160 | tf_op jit(solution)/shard_map/ppermute | solution.py:31
  22.9 5.1 %collective-permute-start.3 = (bf16[3,1,133,1024]{3,2,1,0:T(8,128)(2,1)}, bf16[3,1,133,1024]{3,2,1,0:T(8,128)(2,1)S(1)}, u32[]{:S(2)}, u32[]{:S(2)}) collective-permute-start(bf16[3,1,133,1024]{3,2,1,0:T(8,128)(2,1)} %pad_maximum_fusion.1), channel_id=1, source_target_pairs={{1,0},{2,1},{3,2},{5,4},{6,5},{7,6},{9,8},{10,9},{11,10},{13,12},{... | collective-permute-start | bytes 2451464 | tf_op jit(solution)/shard_map/ppermute | solution.py:34
  24.2 5.2 %collective-permute-start.2 = (bf16[3,1,133,1024]{3,2,1,0:T(8,128)(2,1)}, bf16[3,1,133,1024]{3,2,1,0:T(8,128)(2,1)S(1)}, u32[]{:S(2)}, u32[]{:S(2)}) collective-permute-start(bf16[3,1,133,1024]{3,2,1,0:T(8,128)(2,1)} %pad_maximum_fusion.1), channel_id=1, source_target_pairs={{0,1},{1,2},{2,3},{4,5},{5,6},{6,7},{8,9},{9,10},{10,11},{12,13},{... | collective-permute-start | bytes 2451464 | tf_op jit(solution)/shard_map/ppermute | solution.py:31
  60.4 76.8 %copy-start.3 = (f32[20]{0:T(128)S(1)}, f32[20]{0:T(128)}, u32[]{:S(2)}) copy-start(f32[20]{0:T(128)} %constant.131) | copy-start | bytes 244
  60.5 77.5 %copy-start.2 = (f32[20]{0:T(128)S(1)}, f32[20]{0:T(128)}, u32[]{:S(2)}) copy-start(f32[20]{0:T(128)} %constant.133) | copy-start | bytes 244

commit v4 on v2

--- a/solution.py
+++ b/solution.py
@@ -65,9 +65,8 @@
     return ranks(strip * (4 * PATCH) + position_y + 2 * PATCH * dead)
 
 
-def pair_kernel(edge_sq, groups, chunk, class_ref, lens_ref, x_ref, y_ref, source_ref, catalog_ref, out_ref, crit, sums):
+def pair_kernel(edge_sq, groups, chunk, tile, order_ref, start_ref, lens_ref, x_ref, y_ref, source_ref, catalog_ref, out_ref, crit, sums):
     patches, _, width = source_ref.shape
-    tile = out_ref.shape[2]
     tiles = out_ref.shape[0]
     pieces = width // chunk
 
@@ -103,36 +102,27 @@
             sums[edge, 0] += signal_sum
             sums[edge, 1] += weight_sum
 
+    ones = jnp.ones((8, 128), jnp.float32)
+
     def tile_step(tile_index, carry):
         sums[...] = jnp.zeros_like(sums)
-
-        def chunk_step(index, inner):
-            chosen = class_ref[tile_index, index]
-            for number, first_edge in enumerate(groups):
-                @pl.when(chosen == number)
-                def _():
-                    visit(first_edge, tile_index, index // pieces, index % pieces)
-            return inner
-
-        lax.fori_loop(0, patches * pieces, chunk_step, 0)
-        totals = jnp.sum(sums[...], axis=3)
-        out_ref[tile_index] = jnp.concatenate(
-            [totals[1:, 0] - totals[:-1, 0], totals[1:, 1] - totals[:-1, 1]], axis=0
+        for number, first_edge in enumerate(groups):
+            def chunk_step(place, inner, first_edge=first_edge):
+                index = order_ref[tile_index, place]
+                visit(first_edge, tile_index, index // pieces, index % pieces)
+                return inner
+
+            lax.fori_loop(start_ref[tile_index, number], start_ref[tile_index, number + 1], chunk_step, 0)
+        out_ref[tile_index] = lax.dot_general(
+            ones,
+            sums[...].reshape(-1, 128),
+            (((1,), (1,)), ((), ())),
+            precision=lax.Precision.HIGHEST,
+            preferred_element_type=jnp.float32,
         )
         return carry
 
-    def guarded_step(tile_index, carry):
-        @pl.when(class_ref[tile_index, patches * pieces] > 0)
-        def _():
-            tile_step(tile_index, 0)
-
-        @pl.when(class_ref[tile_index, patches * pieces] <= 0)
-        def _():
-            out_ref[tile_index] = jnp.zeros(out_ref.shape[1:], jnp.float32)
-
-        return carry
-
-    lax.fori_loop(0, tiles, guarded_step, 0)
+    lax.fori_loop(0, tiles, tile_step, 0)
 
 
 def exchange_sum_kernel(table_ref, out_ref, first, partial, second, send_one, recv_one, send_two, recv_two):
@@ -219,8 +209,7 @@
     lens_total = lens_block.shape[3]
     tile = 32
     chunk = 256
-    pieces = width // chunk
-    groups = (0, 13, 17, 20)
+    groups = (0, 8, 12, 14, 17, 18, 20)
     live_count = lens_count[0, 0]
 
     sources = source_block[0, 0]
@@ -287,13 +276,20 @@
     nearest_sq = gap_x * gap_x + gap_y * gap_y
     classes = sum((nearest_sq >= edge_sq[first - 1]).astype(jnp.int32) for first in groups[1:])
     classes = classes + (nearest_sq >= edge_sq[-1]).astype(jnp.int32)
-    live_tile = (jnp.arange(lens_total // tile, dtype=jnp.int32) * tile < live_count).astype(jnp.int32)
-    classes = jnp.concatenate([classes, live_tile[:, None]], axis=1)
+    live_tile = jnp.arange(lens_total // tile, dtype=jnp.int32) * tile < live_count
+    classes = jnp.where(live_tile[:, None], classes, len(groups))
+    chunks = classes.shape[1]
+    chunk_ids = jnp.arange(chunks, dtype=jnp.int32)
+    unique = classes * chunks + chunk_ids[None, :]
+    place = jnp.sum((unique[:, None, :] < unique[:, :, None]).astype(jnp.int32), axis=2)
+    order = jnp.sum(jnp.where(place[:, None, :] == chunk_ids[None, :, None], chunk_ids[None, None, :], 0), axis=2)
+    levels = jnp.arange(len(groups) + 1, dtype=jnp.int32)
+    starts = jnp.sum((classes[:, None, :] < levels[None, :, None]).astype(jnp.int32), axis=2)
 
     totals = pl.pallas_call(
-        functools.partial(pair_kernel, edge_sq, groups, chunk),
-        out_shape=jax.ShapeDtypeStruct((lens_total // tile, 2 * NBIN, tile), jnp.float32),
-        in_specs=[pl.BlockSpec(memory_space=pltpu.SMEM)] + [pl.BlockSpec(memory_space=pltpu.VMEM)] * 5,
+        functools.partial(pair_kernel, edge_sq, groups, chunk, tile),
+        out_shape=jax.ShapeDtypeStruct((lens_total // tile, 8, 2 * (NBIN + 1) * tile), jnp.float32),
+        in_specs=[pl.BlockSpec(memory_space=pltpu.SMEM)] * 2 + [pl.BlockSpec(memory_space=pltpu.VMEM)] * 5,
         out_specs=pl.BlockSpec(memory_space=pltpu.VMEM),
         scratch_shapes=[
             pltpu.VMEM((9, lens_total, width), jnp.float32),
@@ -301,14 +297,17 @@
         ],
         compiler_params=pltpu.CompilerParams(vmem_limit_bytes=48 * 2**20),
     )(
-        classes,
+        order,
+        starts,
         lens_kernel,
         jnp.broadcast_to(lens_x[:, None], (lens_total, 128)),
         jnp.broadcast_to(lens_y[:, None], (lens_total, 128)),
         beside_all[:, :pdf_bins],
         rows,
     )
-    per_lens = jnp.transpose(totals, (0, 2, 1)).reshape(lens_total, 2 * NBIN)
+    below = totals[:, 0].reshape(-1, NBIN + 1, 2, tile)
+    per_bin = below[:, 1:] - below[:, :-1]
+    per_lens = jnp.transpose(per_bin, (0, 3, 2, 1)).reshape(lens_total, 2 * NBIN)
     per_lens = jnp.where((slots < live_count)[:, None], per_lens, 0.0)
     count_ra, count_dec = lax.axis_size("ra"), lax.axis_size("dec")
     region_table = jax.ops.segment_sum(per_lens, segment, num_segments=REG_DEV * count_ra * count_dec * SAMPLES)

time: 108 us -> 101 us (0.935)
  Pallas kernels: 69.9 us -> 59.6 us
  other arithmetic: 10.2 us -> 12.1 us
    pallas_call x1, Pallas kernels: 52.7 us -> 25 us  [exchange_sum(): pl.pallas_call(exchange_sum_kernel, out_shape=jax.ShapeDtypeStruct((rows,...]
    pallas_call x1, Pallas kernels: 17.2 us -> 34.6 us  [on_device(): pl.pallas_call(functools.partial(pair_kernel, edge_sq, groups, chunk, til...]
    reduce_sum x0 -> x3, other arithmetic: none -> 1.83 us  [the longest x1 0.79 us: on_device(): jnp.sum((unique[:, None, :] < unique[:, :, None]).astype(jnp.int32), axis=2)]
  transfers between devices with their start and end apart: 4 -> 4, of which waited for: 4 -> 4; matrix products, arithmetic and copies ran while one was open for 3% -> 4% of each run, Pallas kernels for 0% -> 0%
where the time goes in v4:
time: 101 us
  Pallas kernels  59.6 us (59%)
  other arithmetic  12.1 us (12%)
  waiting for transfers between devices  11.5 us (11%)
  starting transfers between devices  8.72 us (9%)
  local copies, waits for them, and re-layouts  3.79 us (4%)
  matrix products  3.08 us (3%)
  between operations  1.62 us (2%)
    pallas_call x1, Pallas kernels, on_device(): pl.pallas_call(functools.partial(pair_kernel, edge_sq, groups, chunk, til...  34.6 us
    pallas_call x1, Pallas kernels, exchange_sum(): pl.pallas_call(exchange_sum_kernel, out_shape=jax.ShapeDtypeStruct((rows,...  25 us
    ppermute x2, waiting for transfers between devices, extended(): lax.ppermute(lax.slice_in_dim(block, 0, width, axis=dim), axis, backward)  6.24 us
    ppermute x2, waiting for transfers between devices, extended(): lax.ppermute(lax.slice_in_dim(block, block.shape[dim] - width, None, axis...  5.3 us
    ppermute x2, starting transfers between devices, extended(): lax.ppermute(lax.slice_in_dim(block, 0, width, axis=dim), axis, backward)  4.39 us
    ppermute x2, starting transfers between devices, extended(): lax.ppermute(lax.slice_in_dim(block, block.shape[dim] - width, None, axis...  4.32 us
    scatter-add x1, other arithmetic, on_device(): jax.ops.segment_sum(per_lens, segment, num_segments=REG_DEV * count_ra *...  2.51 us
  transfers between devices with their start and end apart: 4, of which 4 were waited for; matrix products, arithmetic and copies ran while one was open for 4% of the time, Pallas kernels for 0%

profile of v4, /device:TPU:0, one launch (start us, length us, event | category | flops | bytes accessed | tf_op | source)
XLA Modules:
  0.0 100.5 jit_solution(11385178935987227900)
XLA Ops:
  0.6 0.7 convert_multiply_fusion
  1.4 0.7 slice_convert_fusion.2
  2.1 0.6 convert_reduce_fusion.1
  2.7 0.6 convert_reduce_fusion
  3.3 1.8 %fusion.3 = bf16[1,1,133,1024]{3,2,1,0:T(8,128)(2,1)S(1)} fusion(s32[1024]{0:T(1024)S(1)} %convert_reduce_fusion, bf16[1,1,133,1024]{3,2,1,0:T(8,128)(2,1)} %param.10), kind=kOutput, calls=%fused_computation.8 | convolution fusion | flops 280105984 | bytes 548864 | tf_op jit(solution)/shard_map/dot_general | solution.py:220
  5.1 3.0 %collective-permute-start = (bf16[1,1,133,1024]{3,2,1,0:T(8,128)(2,1)S(1)}, bf16[1,1,133,1024]{3,2,1,0:T(8,128)(2,1)S(1)}, u32[]{:S(2)}, u32[]{:S(2)}) collective-permute-start(bf16[1,1,133,1024]{3,2,1,0:T(8,128)(2,1)S(1)} %fusion.3), channel_id=1, source_target_pairs={{0,4},{4,8},{8,12},{12,16},{16,20},{20,24},{24,28},{28,0},{1,5},{5... | collective-permute-start | bytes 817160 | tf_op jit(solution)/shard_map/ppermute | solution.py:31
  8.1 3.1 %collective-permute-start.1 = (bf16[1,1,133,1024]{3,2,1,0:T(8,128)(2,1)S(1)}, bf16[1,1,133,1024]{3,2,1,0:T(8,128)(2,1)S(1)}, u32[]{:S(2)}, u32[]{:S(2)}) collective-permute-start(bf16[1,1,133,1024]{3,2,1,0:T(8,128)(2,1)S(1)} %fusion.3), channel_id=1, source_target_pairs={{4,0},{8,4},{12,8},{16,12},{20,16},{24,20},{28,24},{0,28},{5,1},{9... | collective-permute-start | bytes 817160 | tf_op jit(solution)/shard_map/ppermute | solution.py:34
  11.8 0.8 slice_convert_fusion.4
  12.6 0.2 convert_reduce_fusion.3
  12.9 0.3 convert_reduce_fusion.2
  13.5 1.3 %fusion.4 = f32[512,130]{0,1:T(8,128)S(1)} fusion(s32[512]{0:T(512)S(1)} %convert_reduce_fusion.2, bf16[1,1,130,512]{3,2,1,0:T(8,128)(2,1)} %param.6), kind=kOutput, calls=%fused_computation.11 | convolution fusion | flops 68419584 | bytes 401408 | tf_op jit(solution)/shard_map/dot_general | solution.py:232
  14.8 5.2 %collective-permute-done = bf16[1,1,133,1024]{3,2,1,0:T(8,128)(2,1)S(1)} collective-permute-done((bf16[1,1,133,1024]{3,2,1,0:T(8,128)(2,1)S(1)}, bf16[1,1,133,1024]{3,2,1,0:T(8,128)(2,1)S(1)}, u32[]{:S(2)}, u32[]{:S(2)}) %collective-permute-start) | collective-permute-done | bytes 272416 | tf_op jit(solution)/shard_map/ppermute | solution.py:31
  20.0 2.2 %collective-permute-done.1 = bf16[1,1,133,1024]{3,2,1,0:T(8,128)(2,1)S(1)} collective-permute-done((bf16[1,1,133,1024]{3,2,1,0:T(8,128)(2,1)S(1)}, bf16[1,1,133,1024]{3,2,1,0:T(8,128)(2,1)S(1)}, u32[]{:S(2)}, u32[]{:S(2)}) %collective-permute-start.1) | collective-permute-done | bytes 272416 | tf_op jit(solution)/shard_map/ppermute | solution.py:34
  22.2 1.0 pad_maximum_fusion.1
  23.2 1.3 %collective-permute-start.2 = (bf16[3,1,133,1024]{3,2,1,0:T(8,128)(2,1)}, bf16[3,1,133,1024]{3,2,1,0:T(8,128)(2,1)S(1)}, u32[]{:S(2)}, u32[]{:S(2)}) collective-permute-start(bf16[3,1,133,1024]{3,2,1,0:T(8,128)(2,1)} %pad_maximum_fusion.1), channel_id=1, source_target_pairs={{0,1},{1,2},{2,3},{4,5},{5,6},{6,7},{8,9},{9,10},{10,11},{12,13},{... | collective-permute-start | bytes 2451464 | tf_op jit(solution)/shard_map/ppermute | solution.py:31
  24.5 1.3 %collective-permute-start.3 = (bf16[3,1,133,1024]{3,2,1,0:T(8,128)(2,1)}, bf16[3,1,133,1024]{3,2,1,0:T(8,128)(2,1)S(1)}, u32[]{:S(2)}, u32[]{:S(2)}) collective-permute-start(bf16[3,1,133,1024]{3,2,1,0:T(8,128)(2,1)} %pad_maximum_fusion.1), channel_id=1, source_target_pairs={{1,0},{2,1},{3,2},{5,4},{6,5},{7,6},{9,8},{10,9},{11,10},{13,12},{... | collective-permute-start | bytes 2451464 | tf_op jit(solution)/shard_map/ppermute | solution.py:34
  26.6 4.0 %collective-permute-done.3 = bf16[3,1,133,1024]{3,2,1,0:T(8,128)(2,1)S(1)} collective-permute-done((bf16[3,1,133,1024]{3,2,1,0:T(8,128)(2,1)}, bf16[3,1,133,1024]{3,2,1,0:T(8,128)(2,1)S(1)}, u32[]{:S(2)}, u32[]{:S(2)}) %collective-permute-start.3) | collective-permute-done | bytes 817184 | tf_op jit(solution)/shard_map/ppermute | solution.py:34
  30.7 0.3 pad_maximum_fusion
  31.0 0.2 slice.87.source_ref
  31.3 0.3 fusion.43
  32.2 0.8 convert_reduce_fusion.4
  33.1 0.7 select_reduce_fusion.1
  33.8 0.4 convert_reduce_fusion.5.start_ref
  34.3 0.5 stack.5.catalog_ref
  35.0 34.6 %shard_map.77 = f32[16,8,1344]{2,1,0:T(8,128)S(1)} custom-call(s32[16,36]{1,0:T(8,128)S(1)} %copy.35.order_ref, s32[16,8]{1,0:T(8,128)S(1)} %convert_reduce_fusion.5.start_ref, bf16[512,128]{1,0:T(8,128)(2,1)S(1)} %copy.41.lens_ref, f32[512,128]{1,0:T(8,128)S(1)} %broadcast_in_dim.109.x_ref, f32[512,128]{1,0:T(8,128)S(1)} %broadcast_in_dim.111.y_ref, ...), custom_call_target="tpu_custom_call" | custom-call | tf_op jit(solution)/shard_map/pallas_call | solution.py:289
  69.6 0.2 slice_reduce_fusion
  69.9 0.3 reshape_squeeze.11
  70.7 2.5 %scatter_custom_fusion = f32[2048,40]{1,0:T(8,128)S(1)} fusion(s32[512]{0:T(512)S(1)} %select_reduce_fusion, f32[512,40]{1,0:T(8,128)S(1)} %copy.38, f32[]{:T(128)} %constant.105.clone.1), kind=kCustom, calls=%fused_computation.16 | custom fusion | flops 20480 | bytes 327684 | tf_op jit(solution)/shard_map/scatter-add | solution.py:313
  73.3 0.7 reshape.794.table_ref
  74.0 25.0 %shard_map.78 = f32[20,128]{1,0:T(8,128)S(1)} custom-call(f32[4,8,20,128]{3,2,1,0:T(8,128)S(1)} %reshape.794.table_ref), custom_call_target="tpu_custom_call" | custom-call | tf_op jit(solution)/shard_map/pallas_call | solution.py:185
  99.3 0.6 broadcast_multiply_fusion
  99.9 0.6 broadcast_multiply_fusion.1
  (48 shorter events, 3.0 us)
Async XLA Ops:
  1.4 24.9 %copy-start = (s32[1,1,512]{2,1,0:T(1,128)S(1)}, s32[1,1,512]{2,1,0:T(1,128)}, u32[]{:S(2)}) copy-start(s32[1,1,512]{2,1,0:T(1,128)} %param.9) | copy-start | bytes 6148
  1.4 24.9 %copy-start.1 = (s32[1,1,512]{2,1,0:T(1,128)S(1)}, s32[1,1,512]{2,1,0:T(1,128)}, u32[]{:S(2)}) copy-start(s32[1,1,512]{2,1,0:T(1,128)} %param.8) | copy-start | bytes 6148
  5.1 14.9 %collective-permute-start = (bf16[1,1,133,1024]{3,2,1,0:T(8,128)(2,1)S(1)}, bf16[1,1,133,1024]{3,2,1,0:T(8,128)(2,1)S(1)}, u32[]{:S(2)}, u32[]{:S(2)}) collective-permute-start(bf16[1,1,133,1024]{3,2,1,0:T(8,128)(2,1)S(1)} %fusion.3), channel_id=1, source_target_pairs={{0,4},{4,8},{8,12},{12,16},{16,20},{20,24},{24,28},{28,0},{1,5},{5... | collective-permute-start | bytes 817160 | tf_op jit(solution)/shard_map/ppermute | solution.py:31
  8.1 14.1 %collective-permute-start.1 = (bf16[1,1,133,1024]{3,2,1,0:T(8,128)(2,1)S(1)}, bf16[1,1,133,1024]{3,2,1,0:T(8,128)(2,1)S(1)}, u32[]{:S(2)}, u32[]{:S(2)}) collective-permute-start(bf16[1,1,133,1024]{3,2,1,0:T(8,128)(2,1)S(1)} %fusion.3), channel_id=1, source_target_pairs={{4,0},{8,4},{12,8},{16,12},{20,16},{24,20},{28,24},{0,28},{5,1},{9... | collective-permute-start | bytes 817160 | tf_op jit(solution)/shard_map/ppermute | solution.py:34
  23.2 3.5 %collective-permute-start.2 = (bf16[3,1,133,1024]{3,2,1,0:T(8,128)(2,1)}, bf16[3,1,133,1024]{3,2,1,0:T(8,128)(2,1)S(1)}, u32[]{:S(2)}, u32[]{:S(2)}) collective-permute-start(bf16[3,1,133,1024]{3,2,1,0:T(8,128)(2,1)} %pad_maximum_fusion.1), channel_id=1, source_target_pairs={{0,1},{1,2},{2,3},{4,5},{5,6},{6,7},{8,9},{9,10},{10,11},{12,13},{... | collective-permute-start | bytes 2451464 | tf_op jit(solution)/shard_map/ppermute | solution.py:31
  24.5 6.2 %collective-permute-start.3 = (bf16[3,1,133,1024]{3,2,1,0:T(8,128)(2,1)}, bf16[3,1,133,1024]{3,2,1,0:T(8,128)(2,1)S(1)}, u32[]{:S(2)}, u32[]{:S(2)}) collective-permute-start(bf16[3,1,133,1024]{3,2,1,0:T(8,128)(2,1)} %pad_maximum_fusion.1), channel_id=1, source_target_pairs={{1,0},{2,1},{3,2},{5,4},{6,5},{7,6},{9,8},{10,9},{11,10},{13,12},{... | collective-permute-start | bytes 2451464 | tf_op jit(solution)/shard_map/ppermute | solution.py:34
  70.3 29.0 %copy-start.3 = (f32[20]{0:T(128)S(1)}, f32[20]{0:T(128)}, u32[]{:S(2)}) copy-start(f32[20]{0:T(128)} %constant.140) | copy-start | bytes 244
  70.3 29.6 %copy-start.2 = (f32[20]{0:T(128)S(1)}, f32[20]{0:T(128)}, u32[]{:S(2)}) copy-start(f32[20]{0:T(128)} %constant.138) | copy-start | bytes 244

commit v5 on v4

--- a/solution.py
+++ b/solution.py
@@ -67,7 +67,6 @@
 
 def pair_kernel(edge_sq, groups, chunk, tile, order_ref, start_ref, lens_ref, x_ref, y_ref, source_ref, catalog_ref, out_ref, crit, sums):
     patches, _, width = source_ref.shape
-    tiles = out_ref.shape[0]
     pieces = width // chunk
 
     def crit_step(patch, carry):
@@ -102,7 +101,7 @@
             sums[edge, 0] += signal_sum
             sums[edge, 1] += weight_sum
 
-    ones = jnp.ones((8, 128), jnp.float32)
+    ones = jnp.ones((8, 256), jnp.bfloat16)
 
     def tile_step(tile_index, carry):
         sums[...] = jnp.zeros_like(sums)
@@ -113,16 +112,18 @@
                 return inner
 
             lax.fori_loop(start_ref[tile_index, number], start_ref[tile_index, number + 1], chunk_step, 0)
+        per_bin = (sums[1:] - sums[:-1]).reshape(-1, 128)
+        high = per_bin.astype(jnp.bfloat16)
+        low = (per_bin - high.astype(jnp.float32)).astype(jnp.bfloat16)
         out_ref[tile_index] = lax.dot_general(
             ones,
-            sums[...].reshape(-1, 128),
+            jnp.concatenate([high, low], axis=1),
             (((1,), (1,)), ((), ())),
-            precision=lax.Precision.HIGHEST,
             preferred_element_type=jnp.float32,
         )
         return carry
 
-    lax.fori_loop(0, tiles, tile_step, 0)
+    lax.fori_loop(0, start_ref[0, len(groups) + 1], tile_step, 0)
 
 
 def exchange_sum_kernel(table_ref, out_ref, first, partial, second, send_one, recv_one, send_two, recv_two):
@@ -285,10 +286,12 @@
     order = jnp.sum(jnp.where(place[:, None, :] == chunk_ids[None, :, None], chunk_ids[None, None, :], 0), axis=2)
     levels = jnp.arange(len(groups) + 1, dtype=jnp.int32)
     starts = jnp.sum((classes[:, None, :] < levels[None, :, None]).astype(jnp.int32), axis=2)
+    live_tiles = jnp.broadcast_to(jnp.sum(live_tile.astype(jnp.int32)), (lens_total // tile, 1))
+    starts = jnp.concatenate([starts, live_tiles], axis=1)
 
     totals = pl.pallas_call(
         functools.partial(pair_kernel, edge_sq, groups, chunk, tile),
-        out_shape=jax.ShapeDtypeStruct((lens_total // tile, 8, 2 * (NBIN + 1) * tile), jnp.float32),
+        out_shape=jax.ShapeDtypeStruct((lens_total // tile, 8, 2 * NBIN * tile), jnp.float32),
         in_specs=[pl.BlockSpec(memory_space=pltpu.SMEM)] * 2 + [pl.BlockSpec(memory_space=pltpu.VMEM)] * 5,
         out_specs=pl.BlockSpec(memory_space=pltpu.VMEM),
         scratch_shapes=[
@@ -305,8 +308,7 @@
         beside_all[:, :pdf_bins],
         rows,
     )
-    below = totals[:, 0].reshape(-1, NBIN + 1, 2, tile)
-    per_bin = below[:, 1:] - below[:, :-1]
+    per_bin = totals[:, 0].reshape(-1, NBIN, 2, tile)
     per_lens = jnp.transpose(per_bin, (0, 3, 2, 1)).reshape(lens_total, 2 * NBIN)
     per_lens = jnp.where((slots < live_count)[:, None], per_lens, 0.0)
     count_ra, count_dec = lax.axis_size("ra"), lax.axis_size("dec")

time: 101 us -> 94.8 us (0.939)
  Pallas kernels: 59.6 us -> 53.9 us
    pallas_call x1, Pallas kernels: 34.6 us -> 13.3 us  [on_device(): pl.pallas_call(functools.partial(pair_kernel, edge_sq, groups, chunk, til...]
    pallas_call x1, Pallas kernels: 25 us -> 40.6 us  [exchange_sum(): pl.pallas_call(exchange_sum_kernel, out_shape=jax.ShapeDtypeStruct((rows,...]
  transfers between devices with their start and end apart: 4 -> 4, of which waited for: 4 -> 3; matrix products, arithmetic and copies ran while one was open for 4% -> 4% of each run, Pallas kernels for 0% -> 0%
where the time goes in v5:
time: 94.8 us; the launch traced here: 95.2 us
  Pallas kernels  53.9 us (57%)
  other arithmetic  12.6 us (13%)
  waiting for transfers between devices  10.9 us (11%)
  starting transfers between devices  8.71 us (9%)
  local copies, waits for them, and re-layouts  4.33 us (5%)
  matrix products  3.09 us (3%)
  between operations  1.61 us (2%)
    pallas_call x1, Pallas kernels, exchange_sum(): pl.pallas_call(exchange_sum_kernel, out_shape=jax.ShapeDtypeStruct((rows,...  40.6 us
    pallas_call x1, Pallas kernels, on_device(): pl.pallas_call(functools.partial(pair_kernel, edge_sq, groups, chunk, til...  13.3 us
    ppermute x2, waiting for transfers between devices, extended(): lax.ppermute(lax.slice_in_dim(block, 0, width, axis=dim), axis, backward)  5.73 us
    ppermute x2, waiting for transfers between devices, extended(): lax.ppermute(lax.slice_in_dim(block, block.shape[dim] - width, None, axis...  5.19 us
    ppermute x2, starting transfers between devices, extended(): lax.ppermute(lax.slice_in_dim(block, 0, width, axis=dim), axis, backward)  4.39 us
    ppermute x2, starting transfers between devices, extended(): lax.ppermute(lax.slice_in_dim(block, block.shape[dim] - width, None, axis...  4.32 us
    scatter-add x1, other arithmetic, on_device(): jax.ops.segment_sum(per_lens, segment, num_segments=REG_DEV * count_ra *...  2.51 us
  transfers between devices with their start and end apart: 4, of which 3 were waited for; matrix products, arithmetic and copies ran while one was open for 4% of the time, Pallas kernels for 0%

profile of v5, /device:TPU:0, one launch (start us, length us, event | category | flops | bytes accessed | tf_op | source)
XLA Modules:
  0.0 95.2 jit_solution(15051787827268399158)
XLA Ops:
  0.6 0.7 convert_multiply_fusion
  1.4 0.7 slice_convert_fusion.2
  2.1 0.6 convert_reduce_fusion.1
  2.7 0.6 convert_reduce_fusion
  3.3 1.8 %fusion.3 = bf16[1,1,133,1024]{3,2,1,0:T(8,128)(2,1)S(1)} fusion(s32[1024]{0:T(1024)S(1)} %convert_reduce_fusion, bf16[1,1,133,1024]{3,2,1,0:T(8,128)(2,1)} %param.10), kind=kOutput, calls=%fused_computation.8 | convolution fusion | flops 280105984 | bytes 548864 | tf_op jit(solution)/shard_map/dot_general | solution.py:221
  5.1 3.0 %collective-permute-start = (bf16[1,1,133,1024]{3,2,1,0:T(8,128)(2,1)S(1)}, bf16[1,1,133,1024]{3,2,1,0:T(8,128)(2,1)S(1)}, u32[]{:S(2)}, u32[]{:S(2)}) collective-permute-start(bf16[1,1,133,1024]{3,2,1,0:T(8,128)(2,1)S(1)} %fusion.3), channel_id=1, source_target_pairs={{0,4},{4,8},{8,12},{12,16},{16,20},{20,24},{24,28},{28,0},{1,5},{5... | collective-permute-start | bytes 817160 | tf_op jit(solution)/shard_map/ppermute | solution.py:31
  8.1 3.1 %collective-permute-start.1 = (bf16[1,1,133,1024]{3,2,1,0:T(8,128)(2,1)S(1)}, bf16[1,1,133,1024]{3,2,1,0:T(8,128)(2,1)S(1)}, u32[]{:S(2)}, u32[]{:S(2)}) collective-permute-start(bf16[1,1,133,1024]{3,2,1,0:T(8,128)(2,1)S(1)} %fusion.3), channel_id=1, source_target_pairs={{4,0},{8,4},{12,8},{16,12},{20,16},{24,20},{28,24},{0,28},{5,1},{9... | collective-permute-start | bytes 817160 | tf_op jit(solution)/shard_map/ppermute | solution.py:34
  11.8 0.8 slice_convert_fusion.4
  12.6 0.2 convert_reduce_fusion.3
  12.9 0.3 convert_reduce_fusion.2
  13.5 1.3 %fusion.4 = f32[512,130]{0,1:T(8,128)S(1)} fusion(s32[512]{0:T(512)S(1)} %convert_reduce_fusion.2, bf16[1,1,130,512]{3,2,1,0:T(8,128)(2,1)} %param.6), kind=kOutput, calls=%fused_computation.11 | convolution fusion | flops 68419584 | bytes 401408 | tf_op jit(solution)/shard_map/dot_general | solution.py:233
  14.8 5.2 %collective-permute-done = bf16[1,1,133,1024]{3,2,1,0:T(8,128)(2,1)S(1)} collective-permute-done((bf16[1,1,133,1024]{3,2,1,0:T(8,128)(2,1)S(1)}, bf16[1,1,133,1024]{3,2,1,0:T(8,128)(2,1)S(1)}, u32[]{:S(2)}, u32[]{:S(2)}) %collective-permute-start) | collective-permute-done | bytes 272416 | tf_op jit(solution)/shard_map/ppermute | solution.py:31
  20.0 2.2 %collective-permute-done.1 = bf16[1,1,133,1024]{3,2,1,0:T(8,128)(2,1)S(1)} collective-permute-done((bf16[1,1,133,1024]{3,2,1,0:T(8,128)(2,1)S(1)}, bf16[1,1,133,1024]{3,2,1,0:T(8,128)(2,1)S(1)}, u32[]{:S(2)}, u32[]{:S(2)}) %collective-permute-start.1) | collective-permute-done | bytes 272416 | tf_op jit(solution)/shard_map/ppermute | solution.py:34
  22.2 1.0 %pad_maximum_fusion.1 = bf16[3,1,133,1024]{3,2,1,0:T(8,128)(2,1)} fusion(bf16[1,1,133,1024]{3,2,1,0:T(8,128)(2,1)S(1)} %collective-permute-done.1, bf16[1,1,133,1024]{3,2,1,0:T(8,128)(2,1)S(1)} %fusion.3, bf16[1,1,133,1024]{3,2,1,0:T(8,128)(2,1)S(1)} %collective-permute-done), kind=kLoop, calls=%fused_computation.14 | loop fusion | flops 817152 | bytes 1634304 | tf_op jit(solution)/shard_map/concatenate | solution.py:35
  23.2 1.3 %collective-permute-start.2 = (bf16[3,1,133,1024]{3,2,1,0:T(8,128)(2,1)}, bf16[3,1,133,1024]{3,2,1,0:T(8,128)(2,1)S(1)}, u32[]{:S(2)}, u32[]{:S(2)}) collective-permute-start(bf16[3,1,133,1024]{3,2,1,0:T(8,128)(2,1)} %pad_maximum_fusion.1), channel_id=1, source_target_pairs={{0,1},{1,2},{2,3},{4,5},{5,6},{6,7},{8,9},{9,10},{10,11},{12,13},{... | collective-permute-start | bytes 2451464 | tf_op jit(solution)/shard_map/ppermute | solution.py:31
  24.5 1.3 %collective-permute-start.3 = (bf16[3,1,133,1024]{3,2,1,0:T(8,128)(2,1)}, bf16[3,1,133,1024]{3,2,1,0:T(8,128)(2,1)S(1)}, u32[]{:S(2)}, u32[]{:S(2)}) collective-permute-start(bf16[3,1,133,1024]{3,2,1,0:T(8,128)(2,1)} %pad_maximum_fusion.1), channel_id=1, source_target_pairs={{1,0},{2,1},{3,2},{5,4},{6,5},{7,6},{9,8},{10,9},{11,10},{13,12},{... | collective-permute-start | bytes 2451464 | tf_op jit(solution)/shard_map/ppermute | solution.py:34
  26.1 0.6 convert_reduce_fusion.6
  27.1 3.5 %collective-permute-done.3 = bf16[3,1,133,1024]{3,2,1,0:T(8,128)(2,1)S(1)} collective-permute-done((bf16[3,1,133,1024]{3,2,1,0:T(8,128)(2,1)}, bf16[3,1,133,1024]{3,2,1,0:T(8,128)(2,1)S(1)}, u32[]{:S(2)}, u32[]{:S(2)}) %collective-permute-start.3) | collective-permute-done | bytes 817184 | tf_op jit(solution)/shard_map/ppermute | solution.py:34
  30.7 0.3 pad_maximum_fusion
  31.3 0.3 fusion.41
  32.2 0.8 convert_reduce_fusion.4
  33.1 0.7 select_reduce_fusion.1
  33.8 0.4 convert_reduce_fusion.5
  34.2 0.7 concatenate.11.start_ref
  34.9 0.5 stack.5.catalog_ref
  35.7 13.3 %shard_map.77 = f32[16,8,1280]{2,1,0:T(8,128)S(1)} custom-call(s32[16,36]{1,0:T(8,128)S(1)} %copy.32.order_ref, s32[16,9]{1,0:T(8,128)S(1)} %concatenate.11.start_ref, bf16[512,128]{1,0:T(8,128)(2,1)S(1)} %copy.37.lens_ref, f32[512,128]{1,0:T(8,128)S(1)} %broadcast_in_dim.110.x_ref, f32[512,128]{1,0:T(8,128)S(1)} %broadcast_in_dim.112.y_ref, ...), custom_call_target="tpu_custom_call" | custom-call | tf_op jit(solution)/shard_map/pallas_call | solution.py:292
  49.2 0.3 reshape_squeeze.11
  49.9 2.5 %scatter_custom_fusion = f32[2048,40]{1,0:T(8,128)S(1)} fusion(s32[512]{0:T(512)S(1)} %select_reduce_fusion, f32[512,40]{1,0:T(8,128)S(1)} %copy.34, f32[]{:T(128)} %constant.105.clone.1), kind=kCustom, calls=%fused_computation.16 | custom fusion | flops 20480 | bytes 327684 | tf_op jit(solution)/shard_map/scatter-add | solution.py:315
  52.4 0.7 reshape.794.table_ref
  53.2 40.6 %shard_map.78 = f32[20,128]{1,0:T(8,128)S(1)} custom-call(f32[4,8,20,128]{3,2,1,0:T(8,128)S(1)} %reshape.794.table_ref), custom_call_target="tpu_custom_call" | custom-call | tf_op jit(solution)/shard_map/pallas_call | solution.py:186
  93.9 0.6 broadcast_multiply_fusion
  94.6 0.6 broadcast_multiply_fusion.1
  (49 shorter events, 3.1 us)
Async XLA Ops:
  2.1 24.8 %copy-start = (s32[1,1,512]{2,1,0:T(1,128)S(1)}, s32[1,1,512]{2,1,0:T(1,128)}, u32[]{:S(2)}) copy-start(s32[1,1,512]{2,1,0:T(1,128)} %param.9) | copy-start | bytes 6148
  2.1 24.8 %copy-start.1 = (s32[1,1,512]{2,1,0:T(1,128)S(1)}, s32[1,1,512]{2,1,0:T(1,128)}, u32[]{:S(2)}) copy-start(s32[1,1,512]{2,1,0:T(1,128)} %param.8) | copy-start | bytes 6148
  5.1 14.9 %collective-permute-start = (bf16[1,1,133,1024]{3,2,1,0:T(8,128)(2,1)S(1)}, bf16[1,1,133,1024]{3,2,1,0:T(8,128)(2,1)S(1)}, u32[]{:S(2)}, u32[]{:S(2)}) collective-permute-start(bf16[1,1,133,1024]{3,2,1,0:T(8,128)(2,1)S(1)} %fusion.3), channel_id=1, source_target_pairs={{0,4},{4,8},{8,12},{12,16},{16,20},{20,24},{24,28},{28,0},{1,5},{5... | collective-permute-start | bytes 817160 | tf_op jit(solution)/shard_map/ppermute | solution.py:31
  8.1 14.1 %collective-permute-start.1 = (bf16[1,1,133,1024]{3,2,1,0:T(8,128)(2,1)S(1)}, bf16[1,1,133,1024]{3,2,1,0:T(8,128)(2,1)S(1)}, u32[]{:S(2)}, u32[]{:S(2)}) collective-permute-start(bf16[1,1,133,1024]{3,2,1,0:T(8,128)(2,1)S(1)} %fusion.3), channel_id=1, source_target_pairs={{4,0},{8,4},{12,8},{16,12},{20,16},{24,20},{28,24},{0,28},{5,1},{9... | collective-permute-start | bytes 817160 | tf_op jit(solution)/shard_map/ppermute | solution.py:34
  23.2 4.0 %collective-permute-start.2 = (bf16[3,1,133,1024]{3,2,1,0:T(8,128)(2,1)}, bf16[3,1,133,1024]{3,2,1,0:T(8,128)(2,1)S(1)}, u32[]{:S(2)}, u32[]{:S(2)}) collective-permute-start(bf16[3,1,133,1024]{3,2,1,0:T(8,128)(2,1)} %pad_maximum_fusion.1), channel_id=1, source_target_pairs={{0,1},{1,2},{2,3},{4,5},{5,6},{6,7},{8,9},{9,10},{10,11},{12,13},{... | collective-permute-start | bytes 2451464 | tf_op jit(solution)/shard_map/ppermute | solution.py:31
  24.5 6.2 %collective-permute-start.3 = (bf16[3,1,133,1024]{3,2,1,0:T(8,128)(2,1)}, bf16[3,1,133,1024]{3,2,1,0:T(8,128)(2,1)S(1)}, u32[]{:S(2)}, u32[]{:S(2)}) collective-permute-start(bf16[3,1,133,1024]{3,2,1,0:T(8,128)(2,1)} %pad_maximum_fusion.1), channel_id=1, source_target_pairs={{1,0},{2,1},{3,2},{5,4},{6,5},{7,6},{9,8},{10,9},{11,10},{13,12},{... | collective-permute-start | bytes 2451464 | tf_op jit(solution)/shard_map/ppermute | solution.py:34
  49.2 44.7 %copy-start.3 = (f32[20]{0:T(128)S(1)}, f32[20]{0:T(128)}, u32[]{:S(2)}) copy-start(f32[20]{0:T(128)} %constant.142) | copy-start | bytes 244
  49.2 45.3 %copy-start.2 = (f32[20]{0:T(128)S(1)}, f32[20]{0:T(128)}, u32[]{:S(2)}) copy-start(f32[20]{0:T(128)} %constant.140) | copy-start | bytes 244

commit v6 on v5

--- a/solution.py
+++ b/solution.py
@@ -209,14 +209,14 @@
     width = source_block.shape[3]
     lens_total = lens_block.shape[3]
     tile = 32
-    chunk = 256
+    chunk = 128
     groups = (0, 8, 12, 14, 17, 18, 20)
     live_count = lens_count[0, 0]
 
     sources = source_block[0, 0]
     source_x = sources[pdf_bins].astype(jnp.int32)
     source_y = sources[pdf_bins + 1].astype(jnp.int32)
-    source_rank = compact_order(source_x, source_y, jnp.zeros_like(source_x), width // 2)
+    source_rank = compact_order(source_x, source_y, jnp.zeros_like(source_x), width // 4)
     picked = (source_rank[:, None] == jnp.arange(width, dtype=jnp.int32)[None, :]).astype(jnp.bfloat16)
     sources = jnp.dot(sources, picked, preferred_element_type=jnp.float32).astype(jnp.bfloat16)
     partial_rows = extended(sources[None, None], (("ra", 0),), 1, True)

time: 94.8 us -> 95.4 us (level); the launches traced: 95.2 us -> 94.8 us
    pallas_call x1, Pallas kernels: 13.3 us -> 29.6 us  [on_device(): pl.pallas_call(functools.partial(pair_kernel, edge_sq, groups, chunk, til...]
    pallas_call x1, Pallas kernels: 40.6 us -> 25.1 us  [exchange_sum(): pl.pallas_call(exchange_sum_kernel, out_shape=jax.ShapeDtypeStruct((rows,...]
where the time goes in v6:
time: 95.4 us; the launch traced here: 94.8 us
  Pallas kernels  54.7 us (57%)
  other arithmetic  11.8 us (12%)
  waiting for transfers between devices  10.9 us (11%)
  starting transfers between devices  8.72 us (9%)
  local copies, waits for them, and re-layouts  4.06 us (4%)
  matrix products  3.08 us (3%)
  between operations  1.59 us (2%)
    pallas_call x1, Pallas kernels, on_device(): pl.pallas_call(functools.partial(pair_kernel, edge_sq, groups, chunk, til...  29.6 us
    pallas_call x1, Pallas kernels, exchange_sum(): pl.pallas_call(exchange_sum_kernel, out_shape=jax.ShapeDtypeStruct((rows,...  25.1 us
    ppermute x2, waiting for transfers between devices, extended(): lax.ppermute(lax.slice_in_dim(block, 0, width, axis=dim), axis, backward)  5.72 us
    ppermute x2, waiting for transfers between devices, extended(): lax.ppermute(lax.slice_in_dim(block, block.shape[dim] - width, None, axis...  5.18 us
    ppermute x2, starting transfers between devices, extended(): lax.ppermute(lax.slice_in_dim(block, 0, width, axis=dim), axis, backward)  4.39 us
    ppermute x2, starting transfers between devices, extended(): lax.ppermute(lax.slice_in_dim(block, block.shape[dim] - width, None, axis...  4.32 us
    scatter-add x1, other arithmetic, on_device(): jax.ops.segment_sum(per_lens, segment, num_segments=REG_DEV * count_ra *...  2.51 us
  transfers between devices with their start and end apart: 4, of which 3 were waited for; matrix products, arithmetic and copies ran while one was open for 4% of the time, Pallas kernels for 0%

profile of v6, /device:TPU:0, one launch (start us, length us, event | category | flops | bytes accessed | tf_op | source)
XLA Modules:
  0.0 94.8 jit_solution(12176337412820259670)
XLA Ops:
  0.6 0.7 convert_multiply_fusion
  1.4 0.7 slice_convert_fusion.2
  2.1 0.6 convert_reduce_fusion.1
  2.7 0.6 convert_reduce_fusion
  3.3 1.8 %fusion.3 = bf16[1,1,133,1024]{3,2,1,0:T(8,128)(2,1)S(1)} fusion(s32[1024]{0:T(1024)S(1)} %convert_reduce_fusion, bf16[1,1,133,1024]{3,2,1,0:T(8,128)(2,1)} %param.10), kind=kOutput, calls=%fused_computation.8 | convolution fusion | flops 280105984 | bytes 548864 | tf_op jit(solution)/shard_map/dot_general | solution.py:221
  5.1 3.0 %collective-permute-start = (bf16[1,1,133,1024]{3,2,1,0:T(8,128)(2,1)S(1)}, bf16[1,1,133,1024]{3,2,1,0:T(8,128)(2,1)S(1)}, u32[]{:S(2)}, u32[]{:S(2)}) collective-permute-start(bf16[1,1,133,1024]{3,2,1,0:T(8,128)(2,1)S(1)} %fusion.3), channel_id=1, source_target_pairs={{0,4},{4,8},{8,12},{12,16},{16,20},{20,24},{24,28},{28,0},{1,5},{5... | collective-permute-start | bytes 817160 | tf_op jit(solution)/shard_map/ppermute | solution.py:31
  8.1 3.1 %collective-permute-start.1 = (bf16[1,1,133,1024]{3,2,1,0:T(8,128)(2,1)S(1)}, bf16[1,1,133,1024]{3,2,1,0:T(8,128)(2,1)S(1)}, u32[]{:S(2)}, u32[]{:S(2)}) collective-permute-start(bf16[1,1,133,1024]{3,2,1,0:T(8,128)(2,1)S(1)} %fusion.3), channel_id=1, source_target_pairs={{4,0},{8,4},{12,8},{16,12},{20,16},{24,20},{28,24},{0,28},{5,1},{9... | collective-permute-start | bytes 817160 | tf_op jit(solution)/shard_map/ppermute | solution.py:34
  11.9 0.8 slice_convert_fusion.4
  12.6 0.2 convert_reduce_fusion.3
  12.9 0.3 convert_reduce_fusion.2
  13.5 1.3 %fusion.4 = f32[512,130]{0,1:T(8,128)S(1)} fusion(s32[512]{0:T(512)S(1)} %convert_reduce_fusion.2, bf16[1,1,130,512]{3,2,1,0:T(8,128)(2,1)} %param.6), kind=kOutput, calls=%fused_computation.11 | convolution fusion | flops 68419584 | bytes 401408 | tf_op jit(solution)/shard_map/dot_general | solution.py:233
  14.8 5.2 %collective-permute-done = bf16[1,1,133,1024]{3,2,1,0:T(8,128)(2,1)S(1)} collective-permute-done((bf16[1,1,133,1024]{3,2,1,0:T(8,128)(2,1)S(1)}, bf16[1,1,133,1024]{3,2,1,0:T(8,128)(2,1)S(1)}, u32[]{:S(2)}, u32[]{:S(2)}) %collective-permute-start) | collective-permute-done | bytes 272416 | tf_op jit(solution)/shard_map/ppermute | solution.py:31
  20.0 2.2 %collective-permute-done.1 = bf16[1,1,133,1024]{3,2,1,0:T(8,128)(2,1)S(1)} collective-permute-done((bf16[1,1,133,1024]{3,2,1,0:T(8,128)(2,1)S(1)}, bf16[1,1,133,1024]{3,2,1,0:T(8,128)(2,1)S(1)}, u32[]{:S(2)}, u32[]{:S(2)}) %collective-permute-start.1) | collective-permute-done | bytes 272416 | tf_op jit(solution)/shard_map/ppermute | solution.py:34
  22.2 1.0 %pad_maximum_fusion.1 = bf16[3,1,133,1024]{3,2,1,0:T(8,128)(2,1)} fusion(bf16[1,1,133,1024]{3,2,1,0:T(8,128)(2,1)S(1)} %collective-permute-done.1, bf16[1,1,133,1024]{3,2,1,0:T(8,128)(2,1)S(1)} %fusion.3, bf16[1,1,133,1024]{3,2,1,0:T(8,128)(2,1)S(1)} %collective-permute-done), kind=kLoop, calls=%fused_computation.14 | loop fusion | flops 817152 | bytes 1634304 | tf_op jit(solution)/shard_map/concatenate | solution.py:35
  23.2 1.3 %collective-permute-start.2 = (bf16[3,1,133,1024]{3,2,1,0:T(8,128)(2,1)}, bf16[3,1,133,1024]{3,2,1,0:T(8,128)(2,1)S(1)}, u32[]{:S(2)}, u32[]{:S(2)}) collective-permute-start(bf16[3,1,133,1024]{3,2,1,0:T(8,128)(2,1)} %pad_maximum_fusion.1), channel_id=1, source_target_pairs={{0,1},{1,2},{2,3},{4,5},{5,6},{6,7},{8,9},{9,10},{10,11},{12,13},{... | collective-permute-start | bytes 2451464 | tf_op jit(solution)/shard_map/ppermute | solution.py:31
  24.5 1.3 %collective-permute-start.3 = (bf16[3,1,133,1024]{3,2,1,0:T(8,128)(2,1)}, bf16[3,1,133,1024]{3,2,1,0:T(8,128)(2,1)S(1)}, u32[]{:S(2)}, u32[]{:S(2)}) collective-permute-start(bf16[3,1,133,1024]{3,2,1,0:T(8,128)(2,1)} %pad_maximum_fusion.1), channel_id=1, source_target_pairs={{1,0},{2,1},{3,2},{5,4},{6,5},{7,6},{9,8},{10,9},{11,10},{13,12},{... | collective-permute-start | bytes 2451464 | tf_op jit(solution)/shard_map/ppermute | solution.py:34
  26.1 0.6 convert_reduce_fusion.6
  27.2 3.5 %collective-permute-done.3 = bf16[3,1,133,1024]{3,2,1,0:T(8,128)(2,1)S(1)} collective-permute-done((bf16[3,1,133,1024]{3,2,1,0:T(8,128)(2,1)}, bf16[3,1,133,1024]{3,2,1,0:T(8,128)(2,1)S(1)}, u32[]{:S(2)}, u32[]{:S(2)}) %collective-permute-start.3) | collective-permute-done | bytes 817184 | tf_op jit(solution)/shard_map/ppermute | solution.py:34
  30.7 0.3 pad_maximum_fusion
  31.0 0.2 slice.79.source_ref
  31.8 0.3 convert_reduce_fusion.5
  32.2 0.5 convert_reduce_fusion.4
  32.7 0.3 select_reduce_fusion.1.order_ref
  33.1 0.7 concatenate.11.start_ref
  33.8 0.5 stack.5.catalog_ref
  34.5 29.6 %shard_map.77 = f32[16,8,1280]{2,1,0:T(8,128)S(1)} custom-call(s32[16,72]{1,0:T(8,128)S(1)} %select_reduce_fusion.1.order_ref, s32[16,9]{1,0:T(8,128)S(1)} %concatenate.11.start_ref, bf16[512,128]{1,0:T(8,128)(2,1)S(1)} %copy.31.lens_ref, f32[512,128]{1,0:T(8,128)S(1)} %broadcast_in_dim.110.x_ref, f32[512,128]{1,0:T(8,128)S(1)} %broadcast_in_dim.112.y_ref, ...), custom_call_target="tpu_custom_call" | custom-call | tf_op jit(solution)/shard_map/pallas_call | solution.py:292
  64.4 0.3 reshape_squeeze.11
  65.0 2.5 %scatter_custom_fusion = f32[2048,40]{1,0:T(8,128)S(1)} fusion(s32[512]{0:T(512)S(1)} %select_reduce_fusion, f32[512,40]{1,0:T(8,128)S(1)} %copy.28, f32[]{:T(128)} %constant.105.clone.1), kind=kCustom, calls=%fused_computation.19 | custom fusion | flops 20480 | bytes 327684 | tf_op jit(solution)/shard_map/scatter-add | solution.py:315
  67.5 0.7 reshape.794.table_ref
  68.3 25.1 %shard_map.78 = f32[20,128]{1,0:T(8,128)S(1)} custom-call(f32[4,8,20,128]{3,2,1,0:T(8,128)S(1)} %reshape.794.table_ref), custom_call_target="tpu_custom_call" | custom-call | tf_op jit(solution)/shard_map/pallas_call | solution.py:186
  93.6 0.6 broadcast_multiply_fusion
  94.2 0.6 broadcast_multiply_fusion.1
  (44 shorter events, 2.7 us)
Async XLA Ops:
  1.4 25.6 %copy-start = (s32[1,1,512]{2,1,0:T(1,128)S(1)}, s32[1,1,512]{2,1,0:T(1,128)}, u32[]{:S(2)}) copy-start(s32[1,1,512]{2,1,0:T(1,128)} %param.9) | copy-start | bytes 6148
  1.4 25.6 %copy-start.1 = (s32[1,1,512]{2,1,0:T(1,128)S(1)}, s32[1,1,512]{2,1,0:T(1,128)}, u32[]{:S(2)}) copy-start(s32[1,1,512]{2,1,0:T(1,128)} %param.8) | copy-start | bytes 6148
  5.1 14.9 %collective-permute-start = (bf16[1,1,133,1024]{3,2,1,0:T(8,128)(2,1)S(1)}, bf16[1,1,133,1024]{3,2,1,0:T(8,128)(2,1)S(1)}, u32[]{:S(2)}, u32[]{:S(2)}) collective-permute-start(bf16[1,1,133,1024]{3,2,1,0:T(8,128)(2,1)S(1)} %fusion.3), channel_id=1, source_target_pairs={{0,4},{4,8},{8,12},{12,16},{16,20},{20,24},{24,28},{28,0},{1,5},{5... | collective-permute-start | bytes 817160 | tf_op jit(solution)/shard_map/ppermute | solution.py:31
  8.1 14.1 %collective-permute-start.1 = (bf16[1,1,133,1024]{3,2,1,0:T(8,128)(2,1)S(1)}, bf16[1,1,133,1024]{3,2,1,0:T(8,128)(2,1)S(1)}, u32[]{:S(2)}, u32[]{:S(2)}) collective-permute-start(bf16[1,1,133,1024]{3,2,1,0:T(8,128)(2,1)S(1)} %fusion.3), channel_id=1, source_target_pairs={{4,0},{8,4},{12,8},{16,12},{20,16},{24,20},{28,24},{0,28},{5,1},{9... | collective-permute-start | bytes 817160 | tf_op jit(solution)/shard_map/ppermute | solution.py:34
  23.2 4.0 %collective-permute-start.2 = (bf16[3,1,133,1024]{3,2,1,0:T(8,128)(2,1)}, bf16[3,1,133,1024]{3,2,1,0:T(8,128)(2,1)S(1)}, u32[]{:S(2)}, u32[]{:S(2)}) collective-permute-start(bf16[3,1,133,1024]{3,2,1,0:T(8,128)(2,1)} %pad_maximum_fusion.1), channel_id=1, source_target_pairs={{0,1},{1,2},{2,3},{4,5},{5,6},{6,7},{8,9},{9,10},{10,11},{12,13},{... | collective-permute-start | bytes 2451464 | tf_op jit(solution)/shard_map/ppermute | solution.py:31
  24.5 6.2 %collective-permute-start.3 = (bf16[3,1,133,1024]{3,2,1,0:T(8,128)(2,1)}, bf16[3,1,133,1024]{3,2,1,0:T(8,128)(2,1)S(1)}, u32[]{:S(2)}, u32[]{:S(2)}) collective-permute-start(bf16[3,1,133,1024]{3,2,1,0:T(8,128)(2,1)} %pad_maximum_fusion.1), channel_id=1, source_target_pairs={{1,0},{2,1},{3,2},{5,4},{6,5},{7,6},{9,8},{10,9},{11,10},{13,12},{... | collective-permute-start | bytes 2451464 | tf_op jit(solution)/shard_map/ppermute | solution.py:34
  64.3 29.2 %copy-start.3 = (f32[20]{0:T(128)S(1)}, f32[20]{0:T(128)}, u32[]{:S(2)}) copy-start(f32[20]{0:T(128)} %constant.141) | copy-start | bytes 244
  64.3 29.9 %copy-start.2 = (f32[20]{0:T(128)S(1)}, f32[20]{0:T(128)}, u32[]{:S(2)}) copy-start(f32[20]{0:T(128)} %constant.139) | copy-start | bytes 244
